TPU v7x, 256 devices: a whole 4x4x8 slice. The times are simulated.
256 devices in a mesh: row: 8 (over x, y_lo), col: 32 (over z, y_hi, core).
Axes of the slice: x: 4, y: 4 (y_hi: 2, y_lo: 2; y = y_hi * 2 + y_lo), z: 8, core: 2. Of those that a mesh axis runs over, the one named last changes fastest.
Arguments:
- activations: bfloat16 [2048, 6144], P('row', 'col'), may hold values from -600 to 600
- norm_gain: bfloat16 [6144], P('col'), may hold values from 0.099609375 to 1.8984375
- in_weight: bfloat16 [6144, 24576], P('row', 'col'), may hold values from -0.078125 to 0.078125
- in_bias: float32 [24576], P('col'), may hold values from -3 to 3
- out_cotangent: bfloat16 [2048, 24576], P('row', 'col'), may hold values from -6 to 6
Outputs:
- hidden: bfloat16 [2048, 24576], P('row', 'col')
- input_grad: bfloat16 [2048, 6144], P('row', 'col')
- weight_grad: float32 [6144, 24576], P('row', 'col')
- bias_grad: float32 [24576], P('col')
- gain_grad: float32 [6144], P('col')
All inputs are finite; a program needn't handle non-finite values.
Results may differ from a plain program's by a relative error of at most 0.023.
Values may be sent and summed in bfloat16 or wider, within the bound.
No kernel may reach another device: no remote copies, remote signals or barrier semaphores. Data moves between devices by JAX's collectives and lax.ppermute only.
A program may use at most 128 MiB of HBM per device.

v0:
```python
import math

import jax
import jax.numpy as jnp
from jax import lax
from jax.sharding import PartitionSpec as P

D = 6144


def gelu_parts(preact):
    coeff = math.sqrt(2.0 / math.pi)
    inner = coeff * (preact + 0.044715 * preact * preact * preact)
    tanh_val = jnp.tanh(inner)
    value = 0.5 * preact * (1.0 + tanh_val)
    slope = 0.5 * (1.0 + tanh_val) + 0.5 * preact * (1.0 - tanh_val * tanh_val) * coeff * (
        1.0 + 3.0 * 0.044715 * preact * preact
    )
    return (value, slope)


def per_device(activations, norm_gain, in_weight, in_bias, out_cotangent):
    gain_wide = norm_gain.astype(jnp.float32)
    widened = activations.astype(jnp.float32)
    row_total, row_squares = lax.psum(
        (jnp.sum(widened, axis=1), jnp.sum(widened * widened, axis=1)), "col"
    )
    average = row_total[:, None] / D
    variance = row_squares[:, None] / D - average * average
    inv_std = lax.rsqrt(variance + 1e-06)
    x_hat = (widened - average) * inv_std
    normed = (x_hat * gain_wide).astype(jnp.bfloat16)
    normed_full = lax.all_gather(normed, "col", axis=1, tiled=True)
    preact = (
        jnp.dot(
            normed_full,
            lax.all_gather(in_weight, "row", axis=0, tiled=True),
            preferred_element_type=jnp.float32,
        )
        + in_bias
    )
    value, slope = gelu_parts(preact)
    hidden = value.astype(jnp.bfloat16)
    pre_grad = (out_cotangent.astype(jnp.float32) * slope).astype(jnp.bfloat16)
    panel_normed = lax.all_to_all(normed_full, "row", split_axis=1, concat_axis=0, tiled=True)
    weight_grad = lax.dot_general(
        panel_normed,
        lax.all_gather(pre_grad, "row", axis=0, tiled=True),
        (((0,), (0,)), ((), ())),
        preferred_element_type=jnp.float32,
    )
    partial_grad = lax.dot_general(
        pre_grad,
        lax.all_gather(in_weight, "row", axis=0, tiled=True),
        (((1,), (1,)), ((), ())),
        preferred_element_type=jnp.float32,
    )
    normed_grad = lax.psum_scatter(
        partial_grad.astype(jnp.bfloat16), "col", scatter_dimension=1, tiled=True
    ).astype(jnp.float32)
    scaled = normed_grad * gain_wide
    first_sum, second_sum = lax.psum(
        (jnp.sum(scaled, axis=1), jnp.sum(scaled * x_hat, axis=1)), "col"
    )
    input_grad = (
        inv_std * (scaled - first_sum[:, None] / D - x_hat * second_sum[:, None] / D)
    ).astype(jnp.bfloat16)
    gain_part = jnp.sum(normed_grad * x_hat, axis=0)
    bias_grad, gain_grad = lax.psum(
        (jnp.sum(pre_grad.astype(jnp.float32), axis=0), gain_part), "row"
    )
    return (hidden, input_grad, weight_grad, bias_grad, gain_grad)


def solution(mesh):
    return jax.shard_map(
        per_device,
        mesh=mesh,
        in_specs=(P("row", "col"), P("col"), P("row", "col"), P("col"), P("row", "col")),
        out_specs=(P("row", "col"), P("row", "col"), P("row", "col"), P("col"), P("col")),
        check_vma=False,
    )
```

profile of v0, /device:TPU:14, one launch (start us, length us, event | category | flops | bytes accessed | tf_op | source)
XLA Modules:
  0.0 589.0 jit_solution(12080463699457185341)
XLA Ops:
  7.2 0.0 all-gather.4.cloned.1.call-start
  7.2 0.7 convert_element_type.31
  7.9 0.9 convert_reduce_fusion.1
  8.8 72.0 %all-reduce.1 = (f32[256]{0:T(256)S(1)}, f32[256]{0:T(256)S(1)}) all-reduce(f32[256]{0:T(256)S(1)} %get-tuple-element.9, f32[256]{0:T(256)S(1)} %get-tuple-element.8), channel_id=1, replica_groups=mesh['row'=8,'col'=32] {'col'}, use_global_device_ids=true, to_apply=%region_3.0 | all-reduce | flops 512 | bytes 4096 | tf_op jit(solution)/shard_map/psum | solution.py:25
  80.9 1.6 fusion.18
  82.5 0.0 all-gather.4.cloned.1.call-update
  82.5 0.0 all-gather.6.cloned.1.call-start
  82.6 0.7 all-gather.6.cloned.1.call-update
  83.3 0.0 reduce-scatter.2.cloned.1.call-start
  83.3 77.2 %all-gather.4.cloned.1.call-done = bf16[256,6144]{0,1:T(8,128)(2,1)} async-done(((bf16[256,192]{0,1:T(8,128)(2,1)}), bf16[256,6144]{0,1:T(8,128)(2,1)}) %all-gather.4.cloned.1.call-update) | async-done | bytes 3145744 | tf_op jit(solution)/shard_map/all_gather | solution.py:33
  160.5 188.9 %all-gather.6.cloned.1.call-done = bf16[6144,768]{1,0:T(8,128)(2,1)} async-done(((bf16[768,768]{1,0:T(8,128)(2,1)}), bf16[6144,768]{1,0:T(8,128)(2,1)}) %all-gather.6.cloned.1.call-update) | async-done | bytes 9437200 | tf_op jit(solution)/shard_map/all_gather | solution.py:37
  349.4 8.4 %convert_reduce_fusion = (f32[768]{0:T(1024)S(1)}, bf16[256,768]{1,0:T(8,128)(2,1)S(1)}, bf16[256,768]{1,0:T(8,128)(2,1)}) fusion(bf16[256,768]{1,0:T(8,128)(2,1)} %param.9, f32[768]{0:T(1024)} %param.8, bf16[256,6144]{0,1:T(8,128)(2,1)} %all-gather.4.cloned.1.call-done, bf16[6144,768]{1,0:T(8,128)(2,1)} %all-gather.6.cloned.1.call-done), kind=kOutput, calls=%fused_computation.11 | convolution fusion | flops 2420833536 | bytes 13768704 | tf_op jit(solution)/shard_map/dot_general | solution.py:35
  357.9 0.0 copy-start.2
  357.9 8.1 %convolution_convert_fusion = bf16[256,6144]{0,1:T(8,128)(2,1)} fusion(bf16[256,768]{1,0:T(8,128)(2,1)S(1)} %get-tuple-element.17, bf16[6144,768]{1,0:T(8,128)(2,1)} %all-gather.6.cloned.1.call-done), kind=kOutput, calls=%fused_computation | convolution fusion | flops 2417491968 | bytes 12976128 | tf_op jit(solution)/shard_map/dot_general | solution.py:52
  366.0 0.0 copy-done.2
  366.0 0.0 copy-start
  366.0 0.0 reduce-scatter.2.cloned.1.call-update
  366.0 0.0 all-gather.8.cloned.1.call-start
  366.1 0.5 all-gather.8.cloned.1.call-update
  366.6 1.3 copy-done
  367.9 2.8 copy.10
  370.7 0.0 copy-start.1
  370.7 7.4 %all-to-all-start = ((bf16[256,8,768]{2,0,1:T(8,128)(2,1)}), bf16[256,8,768]{2,0,1:T(8,128)(2,1)S(1)}, u32[]{:S(2)}, u32[]{:S(2)}) async-start(bf16[256,8,768]{2,0,1:T(8,128)(2,1)} %copy.10), calls=%async_computation.1 | async-start | bytes 6291456 | tf_op jit(solution)/shard_map/all_to_all | solution.py:45
  378.1 113.1 %reduce-scatter.2.cloned.1.call-done = bf16[256,192]{0,1:T(8,128)(2,1)} async-done(((bf16[256,6144]{0,1:T(8,128)(2,1)}), bf16[256,192]{0,1:T(8,128)(2,1)}) %reduce-scatter.2.cloned.1.call-update) | async-done | bytes 98320 | tf_op jit(solution)/shard_map/reduce_scatter | solution.py:58
  491.2 0.0 copy-done.1
  491.2 1.0 fusion.14
  492.3 66.1 %all-reduce = (f32[256]{0:T(256)S(1)}, f32[256]{0:T(256)S(1)}) all-reduce(f32[256]{0:T(256)S(1)} %get-tuple-element.6, f32[256]{0:T(256)S(1)} %get-tuple-element.7), channel_id=1, replica_groups=mesh['row'=8,'col'=32] {'col'}, use_global_device_ids=true, to_apply=%region_8.0 | all-reduce | flops 512 | bytes 4096 | tf_op jit(solution)/shard_map/psum | solution.py:62
  558.4 16.5 %all-reduce.2 = (f32[768]{0:T(1024)}, f32[192]{0:T(256)}) all-reduce(f32[768]{0:T(1024)S(1)} %get-tuple-element.16, f32[192]{0:T(256)S(1)} %get-tuple-element.5), channel_id=1, replica_groups=mesh['row'=8,'col'=32] {'row'}, use_global_device_ids=true, to_apply=%region_10.0 | all-reduce | flops 960 | bytes 7680 | tf_op jit(solution)/shard_map/psum | solution.py:69
  574.8 1.6 fusion.12
  576.5 0.0 all-to-all-done
  576.5 0.0 all-gather.8.cloned.1.call-done
  576.5 6.0 %fusion.22 = f32[768,768]{1,0:T(8,128)} fusion(bf16[2048,768]{1,0:T(8,128)(2,1)S(1)} %bitcast.11, bf16[2048,768]{1,0:T(8,128)(2,1)} %all-gather.8.cloned.1.call-done), kind=kOutput, calls=%fused_computation.35 | convolution fusion | flops 2415919104 | bytes 8650752 | tf_op jit(solution)/shard_map/dot_general | solution.py:46
  (2 shorter events, 0.0 us)
Async XLA Ops:
  7.2 153.3 %all-gather.4.cloned.1.call-start = ((), (), s32[]{:S(2)}) async-start(), calls=%async_computation.2 | async-start | bytes 3244032 | tf_op jit(solution)/shard_map/all_gather | solution.py:33
  82.5 266.9 %all-gather.6.cloned.1.call-start = ((), (), s32[]{:S(2)}) async-start(), calls=%async_computation.3 | async-start | bytes 10616832 | tf_op jit(solution)/shard_map/all_gather | solution.py:37
  83.3 408.0 %reduce-scatter.2.cloned.1.call-start = ((), (), s32[]{:S(2)}) async-start(), calls=%async_computation.4 | async-start | bytes 3244032 | tf_op jit(solution)/shard_map/reduce_scatter | solution.py:58
  357.9 8.1 %copy-start.2 = (bf16[256,768]{1,0:T(8,128)(2,1)}, bf16[256,768]{1,0:T(8,128)(2,1)S(1)}, u32[]{:S(2)}) copy-start(bf16[256,768]{1,0:T(8,128)(2,1)S(1)} %get-tuple-element.17) | copy-start | bytes 1179652
  366.0 1.9 copy-start
  366.0 210.5 %all-gather.8.cloned.1.call-start = ((), (), s32[]{:S(2)}) async-start(), calls=%async_computation.5 | async-start | bytes 3538944 | tf_op jit(solution)/shard_map/all_gather | solution.py:48
  370.7 120.5 %copy-start.1 = (bf16[256,192]{0,1:T(8,128)(2,1)S(1)}, bf16[256,192]{0,1:T(8,128)(2,1)}, u32[]{:S(2)}) copy-start(bf16[256,192]{0,1:T(8,128)(2,1)} %param.5) | copy-start | bytes 294916
  370.7 205.8 %all-to-all-start = ((bf16[256,8,768]{2,0,1:T(8,128)(2,1)}), bf16[256,8,768]{2,0,1:T(8,128)(2,1)S(1)}, u32[]{:S(2)}, u32[]{:S(2)}) async-start(bf16[256,8,768]{2,0,1:T(8,128)(2,1)} %copy.10), calls=%async_computation.1 | async-start | bytes 6291456 | tf_op jit(solution)/shard_map/all_to_all | solution.py:45
Sparse Core Ops, SparseCore 0:
  82.6 77.8 all-gather.3
  162.3 187.0 all-gather.5
  366.1 125.0 reduce-scatter.1
  493.6 71.6 all-gather.7
where the time goes:
time: 592 us; the launch traced here: 589 us
  waiting for transfers between devices  380 us (64%)
  blocking collectives  155 us (26%)
  matrix products  22.5 us (4%)
  between operations  13.8 us (2%)
  starting transfers between devices  7.59 us (1%)
  other arithmetic  5.93 us (1%)
    all_gather x1, waiting for transfers between devices, per_device(): lax.all_gather(in_weight, 'row', axis=0, tiled=True)  189 us
    reduce_scatter x1, waiting for transfers between devices, per_device(): lax.psum_scatter(partial_grad.astype(jnp.bfloat16), 'col', scatter_dimens...  113 us
    all_gather x1, waiting for transfers between devices, per_device(): normed_full = lax.all_gather(normed, 'col', axis=1, tiled=True)  77.2 us
    psum x1, blocking collectives, per_device(): lax.psum((jnp.sum(widened, axis=1), jnp.sum(widened * widened, axis=1)),...  72 us
    psum x1, blocking collectives, per_device(): lax.psum((jnp.sum(scaled, axis=1), jnp.sum(scaled * x_hat, axis=1)), 'col')  66.1 us
    psum x1, blocking collectives, per_device(): lax.psum((jnp.sum(pre_grad.astype(jnp.float32), axis=0), gain_part), 'row')  16.5 us
  transfers between devices with their start and end apart: 5, of which 3 were waited for; matrix products, arithmetic and copies ran while one was open for 1% of the time, Pallas kernels for 0%

commit v1 on v0

v1 whole, which is shorter than its diff:
```python
import functools
import math

import jax
import jax.numpy as jnp
from jax import lax
from jax.experimental import pallas as pl
from jax.experimental.pallas import tpu as pltpu
from jax.sharding import Mesh
from jax.sharding import PartitionSpec as P

D = 6144
PANEL = 768
BLOCK = 192
HALF = 384
TOK = 256
N = 1
T = TOK // N
AXES = ("x", "yl", "z", "yh", "k")
SIZES = (4, 2, 8, 2, 2)
ROW = ("x", "yl")
COL = ("z", "yh", "k")
f32, bf16 = jnp.float32, jnp.bfloat16


def gelu_parts(preact):
    coeff = math.sqrt(2.0 / math.pi)
    inner = coeff * (preact + 0.044715 * preact * preact * preact)
    tanh_val = jnp.tanh(inner)
    value = 0.5 * preact * (1.0 + tanh_val)
    slope = 0.5 * (1.0 + tanh_val) + 0.5 * preact * (1.0 - tanh_val * tanh_val) * coeff * (
        1.0 + 3.0 * 0.044715 * preact * preact
    )
    return (value, slope)


def shift(value, axis, by):
    size = SIZES[AXES.index(axis)]
    return lax.ppermute(value, axis, [(i, (i + by) % size) for i in range(size)])


def transpose_pairs(inverse):
    pairs = []
    for r in range(8):
        for z in range(8):
            for q in range(4):
                here, there = r * 32 + z * 4 + q, z * 32 + r * 4 + q
                pairs.append((there, here) if inverse else (here, there))
    return pairs


def to_all(value, axes, count):
    return lax.all_to_all(
        jnp.broadcast_to(value[None], (count,) + value.shape), axes, 0, 0
    )


def norm_matmul_kernel(idx, own, other, stats, gain, wt, normed, partial):
    first = idx[1] == 0
    a, b = own[0].astype(f32), other[0].astype(f32)
    low, high = jnp.where(first, a, b), jnp.where(first, b, a)
    x = jnp.concatenate([low[:BLOCK], high[:BLOCK], low[BLOCK:], high[BLOCK:]], axis=0)
    average = stats[0, 0:1, :] / D
    variance = stats[0, 1:2, :] / D - average * average
    inv_std = lax.rsqrt(variance + 1e-06)
    n = ((x - average) * inv_std * gain[...]).astype(bf16)
    normed[0] = n
    partial[0] = jnp.dot(wt[...], n, preferred_element_type=f32).astype(bf16)


def norm_matmul(idx, own, other, stats, gain, wt):
    blk = pl.BlockSpec((1, HALF, T), lambda p, s: ((s[0] + 8 - p) % 8, 0, 0))
    out = pl.BlockSpec((1, PANEL, T), lambda p, s: (p, 0, 0))
    return pl.pallas_call(
        norm_matmul_kernel,
        grid_spec=pltpu.PrefetchScalarGridSpec(
            num_scalar_prefetch=1,
            grid=(8,),
            in_specs=[
                blk,
                blk,
                pl.BlockSpec((1, 2, T), lambda p, s: (p, 0, 0)),
                pl.BlockSpec((PANEL, 1), lambda p, s: (0, 0)),
                pl.BlockSpec((PANEL, PANEL), lambda p, s: (0, 0)),
            ],
            out_specs=[out, out],
        ),
        out_shape=[jax.ShapeDtypeStruct((8, PANEL, T), bf16)] * 2,
        compiler_params=pltpu.CompilerParams(vmem_limit_bytes=32 * 2**20),
        cost_estimate=pl.CostEstimate(
            flops=2 * 8 * PANEL * PANEL * T, bytes_accessed=10_000_000, transcendentals=0
        ),
        name="norm_matmul",
    )(idx, own, other, stats, gain, wt)


def back_matmul_kernel(idx, w, grad, mine, theirs):
    first = idx[1] == 0
    dx = jnp.dot(w[...], grad[0], preferred_element_type=f32)
    low = jnp.concatenate([dx[:BLOCK], dx[2 * BLOCK : 3 * BLOCK]], axis=0)
    high = jnp.concatenate([dx[BLOCK : 2 * BLOCK], dx[3 * BLOCK :]], axis=0)
    mine[0] = jnp.where(first, low, high).astype(bf16)
    theirs[0] = jnp.where(first, high, low).astype(bf16)


def back_matmul(idx, w, grad):
    out = pl.BlockSpec((1, HALF, T), lambda p, s: (p, 0, 0))
    return pl.pallas_call(
        back_matmul_kernel,
        grid_spec=pltpu.PrefetchScalarGridSpec(
            num_scalar_prefetch=1,
            grid=(8,),
            in_specs=[
                pl.BlockSpec((PANEL, PANEL), lambda p, s: (0, 0)),
                pl.BlockSpec((1, PANEL, T), lambda p, s: (p, 0, 0)),
            ],
            out_specs=[out, out],
        ),
        out_shape=[jax.ShapeDtypeStruct((8, HALF, T), bf16)] * 2,
        compiler_params=pltpu.CompilerParams(vmem_limit_bytes=32 * 2**20),
        cost_estimate=pl.CostEstimate(
            flops=2 * 8 * PANEL * PANEL * T, bytes_accessed=8_000_000, transcendentals=0
        ),
        name="back_matmul",
    )(idx, w, grad)


def weight_grad_kernel(*refs):
    normed, grads = refs[:N], refs[N : 2 * N]
    w, out, bias, rows = refs[2 * N :]
    step = pl.program_id(0)

    @pl.when(step == 0)
    def _():
        out[...] = jnp.zeros_like(out)
        bias[...] = jnp.zeros_like(bias)

    total = out[...]
    bias_total = bias[...]
    for n, g in zip(normed, grads):
        total = total + lax.dot_general(
            n[0], g[0], (((1,), (1,)), ((), ())), preferred_element_type=f32
        )
        bias_total = bias_total + jnp.sum(g[0].astype(f32), axis=1, keepdims=True)
    out[...] = total
    bias[...] = bias_total

    @pl.when(step == 7)
    def _():
        rows[...] = jnp.sum(out[...] * w[...].astype(f32), axis=1, keepdims=True)


def weight_grads(normed, grads, w):
    blk = pl.BlockSpec((1, PANEL, T), lambda p: (p, 0, 0))
    whole = pl.BlockSpec((PANEL, PANEL), lambda p: (0, 0))
    column = pl.BlockSpec((PANEL, 1), lambda p: (0, 0))
    return pl.pallas_call(
        weight_grad_kernel,
        grid=(8,),
        in_specs=[blk] * (2 * N) + [whole],
        out_specs=[whole, column, column],
        out_shape=[
            jax.ShapeDtypeStruct((PANEL, PANEL), f32),
            jax.ShapeDtypeStruct((PANEL, 1), f32),
            jax.ShapeDtypeStruct((PANEL, 1), f32),
        ],
        compiler_params=pltpu.CompilerParams(vmem_limit_bytes=32 * 2**20),
        cost_estimate=pl.CostEstimate(
            flops=2 * 8 * N * PANEL * PANEL * T, bytes_accessed=10_000_000, transcendentals=0
        ),
        name="weight_grads",
    )(*normed, *grads, w)


def pick(stack, index):
    return lax.dynamic_index_in_dim(stack, index, 0, keepdims=False)


def gather_z(block):
    up = down = block
    got = {0: block}
    for step in range(1, 5):
        up = shift(up, "z", 1)
        got[step] = up
        if step < 4:
            down = shift(down, "z", -1)
            got[8 - step] = down
    return jnp.stack([got[j] for j in range(8)])


def scatter_z(mine, other, z):
    def term(offset):
        i = (z + offset + 8) % 8
        return pick(mine, i).astype(f32) + pick(other, i).astype(f32)

    up, down = term(4).astype(bf16), term(-3).astype(bf16)
    for step in range(1, 4):
        up = shift(up, "z", 1)
        up = (up.astype(f32) + term(4 - step)).astype(bf16)
        down = shift(down, "z", -1)
        if step < 3:
            down = (down.astype(f32) + term(step - 3)).astype(bf16)
    up = shift(up, "z", 1)
    return up.astype(f32) + down.astype(f32) + term(0)


def per_device(activations, norm_gain, in_weight, in_bias, out_cotangent):
    row = lax.axis_index(ROW)
    col = lax.axis_index(COL)
    z, yh, k = lax.axis_index("z"), lax.axis_index("yh"), lax.axis_index("k")
    idx = jnp.stack([z, k]).astype(jnp.int32)

    act_t = activations.T
    wide_t = act_t.astype(f32)
    gain_own = norm_gain.astype(f32)

    parts = jnp.stack([act_t[:, i * T : (i + 1) * T] for i in range(N)])
    parts = lax.ppermute(parts, AXES, transpose_pairs(False))
    swapped = shift(parts, "yh", 1)
    parts = jnp.where(
        yh == 0,
        jnp.concatenate([parts, swapped], axis=1),
        jnp.concatenate([swapped, parts], axis=1),
    )

    small = jnp.concatenate(
        [
            jnp.sum(wide_t, axis=0),
            jnp.sum(wide_t * wide_t, axis=0),
            gain_own,
            jnp.zeros((320,), f32),
        ]
    ).reshape(8, 128)
    smalls = to_all(small, COL, 32).reshape(32, 1024)
    sums = jnp.sum(smalls[:, : 2 * TOK], axis=0)
    gain_panel = lax.dynamic_slice(smalls[:, 512:704], (4 * row, 0), (4, BLOCK)).reshape(PANEL, 1)
    w_wide = in_weight.astype(f32)
    wsum = jnp.sum(w_wide * gain_panel, axis=0)
    more = jnp.concatenate([sums, wsum, jnp.zeros((768,), f32)]).reshape(16, 128)
    mores = to_all(more, ROW, 8).reshape(8, 2048)
    wsum = jnp.sum(mores[:, 512:1280], axis=0)
    stats = mores[:, :512].reshape(8, 2, N, T)

    wt = in_weight.T
    cot_t = out_cotangent.T
    bias_col = in_bias[:, None]
    wsum_col = wsum[:, None]

    normed, hidden, grads, s1, s2 = [], [], [], [], []
    for i in range(N):
        own = gather_z(parts[i])
        other = shift(own, "k", 1)
        n, partial = norm_matmul(idx, own, other, stats[:, :, i], gain_panel, wt)
        normed.append(n)
        recv = lax.all_to_all(partial, ROW, 0, 0)
        linear = jnp.sum(recv.astype(f32), axis=0)
        value, slope = gelu_parts(linear + bias_col)
        hidden.append(value.astype(bf16))
        grad = (cot_t[:, i * T : (i + 1) * T].astype(f32) * slope).astype(bf16)
        wide = grad.astype(f32)
        s1.append(jnp.sum(wide * wsum_col, axis=0))
        s2.append(jnp.sum(wide * linear, axis=0))
        grads.append(to_all(grad, ROW, 8))

    pieces = []
    for i in range(N):
        mine, theirs = back_matmul(idx, in_weight, grads[i])
        total = scatter_z(mine, shift(theirs, "k", 1), z)
        kept = jnp.where(yh == 0, total[:BLOCK], total[BLOCK:])
        sent = jnp.where(yh == 0, total[BLOCK:], total[:BLOCK]).astype(bf16)
        kept = kept + shift(sent, "yh", 1).astype(f32)
        pieces.append(kept.astype(bf16))
    back = lax.ppermute(jnp.stack(pieces), AXES, transpose_pairs(True))
    normed_grad = jnp.concatenate([back[i] for i in range(N)], axis=1).astype(f32)

    weight_grad, bias_grad, rows = weight_grads(normed, grads, in_weight)

    pair = jnp.concatenate(s1 + s2).reshape(4, 128)
    totals = jnp.sum(to_all(pair, COL, 32), axis=0).reshape(2, 1, TOK)
    average = sums[None, :TOK] / D
    variance = sums[None, TOK:] / D - average * average
    inv_std = lax.rsqrt(variance + 1e-06)
    x_hat = (wide_t - average) * inv_std
    scaled = normed_grad * gain_own[:, None]
    input_grad = (inv_std * (scaled - totals[0] / D - x_hat * totals[1] / D)).astype(bf16).T

    rows = jnp.concatenate([rows[:, 0], jnp.zeros((256,), f32)]).reshape(8, 128)
    rows = jnp.sum(to_all(rows, COL, 32), axis=0)
    rows = to_all(rows, ROW, 8).reshape(8, 1024)[:, :PANEL].reshape(32, BLOCK)
    gain_grad = pick(rows, col) / gain_own

    hidden = jnp.concatenate(hidden, axis=1).T
    return (hidden, input_grad, weight_grad, bias_grad[:, 0], gain_grad)


def solution(mesh):
    fine = Mesh(mesh.devices.reshape(SIZES), AXES)
    both = P(ROW, COL)
    return jax.shard_map(
        per_device,
        mesh=fine,
        in_specs=(both, P(COL), both, P(COL), both),
        out_specs=(both, both, both, P(COL), P(COL)),
        check_vma=False,
    )
```

time: 592 us -> 289 us (0.49)
  waiting for transfers between devices: 380 us -> 116 us
  blocking collectives: 155 us -> 40.8 us
  starting transfers between devices: 7.59 us -> 76.5 us
  matrix products: 22.5 us -> 0 us
  Pallas kernels: 0 us -> 19.7 us
  local copies, waits for them, and re-layouts: 4.12 us -> 17.9 us
  between operations: 13.8 us -> 1.02 us
  other arithmetic: 5.93 us -> 16 us
    all_gather x3 -> x0, waiting for transfers between devices: 266 us -> none  [the longest x1 189 us: per_device(): lax.all_gather(in_weight, 'row', axis=0, tiled=True)]
    psum x3 -> x0, blocking collectives: 155 us -> none  [the longest x1 72 us: per_device(): lax.psum((jnp.sum(widened, axis=1), jnp.sum(widened * widened, axis=1)),...]
    reduce_scatter x1 -> x0, waiting for transfers between devices: 113 us -> none  [per_device(): lax.psum_scatter(partial_grad.astype(jnp.bfloat16), 'col', scatter_dimens...]
    all_to_all x1 -> x6, waiting for transfers between devices: 0.01 us -> 63.1 us  [the longest x1 41.3 us: per_device(): recv = lax.all_to_all(partial, ROW, 0, 0)]
    ppermute x0 -> x20, waiting for transfers between devices: none -> 52.8 us  [the longest x18 33.2 us: shift(): lax.ppermute(value, axis, [(i, (i + by) % size) for i in range(size)])]
    all_to_all x0 -> x1, blocking collectives: none -> 40.8 us  [to_all(): lax.all_to_all(jnp.broadcast_to(value[None], (count,) + value.shape), axe...]
    ppermute x0 -> x20, starting transfers between devices: none -> 34.8 us  [the longest x18 22.6 us: shift(): lax.ppermute(value, axis, [(i, (i + by) % size) for i in range(size)])]
    all_to_all x1 -> x6, starting transfers between devices: 7.43 us -> 41.7 us  [the longest x5 34.5 us: to_all(): lax.all_to_all(jnp.broadcast_to(value[None], (count,) + value.shape), axe...]
  transfers between devices with their start and end apart: 5 -> 26, of which waited for: 3 -> 14; matrix products, arithmetic and copies ran while one was open for 1% -> 6% of each run, Pallas kernels for 0% -> 2%
where the time goes in v1:
time: 289 us; the launch traced here: 288 us
  waiting for transfers between devices  116 us (40%)
  starting transfers between devices  76.5 us (26%)
  blocking collectives  40.8 us (14%)
  Pallas kernels  19.7 us (7%)
  local copies, waits for them, and re-layouts  17.9 us (6%)
  other arithmetic  16 us (6%)
    all_to_all x1, waiting for transfers between devices, per_device(): recv = lax.all_to_all(partial, ROW, 0, 0)  41.3 us
    all_to_all x1, blocking collectives, to_all(): lax.all_to_all(jnp.broadcast_to(value[None], (count,) + value.shape), axe...  40.8 us
    all_to_all x5, starting transfers between devices, to_all(): lax.all_to_all(jnp.broadcast_to(value[None], (count,) + value.shape), axe...  34.5 us
    ppermute x18, waiting for transfers between devices, shift(): lax.ppermute(value, axis, [(i, (i + by) % size) for i in range(size)])  33.2 us
    ppermute x18, starting transfers between devices, shift(): lax.ppermute(value, axis, [(i, (i + by) % size) for i in range(size)])  22.6 us
    all_to_all x5, waiting for transfers between devices, to_all(): lax.all_to_all(jnp.broadcast_to(value[None], (count,) + value.shape), axe...  21.9 us
    unnamed x40, local copies, waits for them, and re-layouts  13.3 us
    ppermute x1, waiting for transfers between devices, per_device(): back = lax.ppermute(jnp.stack(pieces), AXES, transpose_pairs(True))  9.88 us
  transfers between devices with their start and end apart: 26, of which 14 were waited for; matrix products, arithmetic and copies ran while one was open for 6% of the time, Pallas kernels for 2%

profile of v1, /device:TPU:14, one launch (start us, length us, event | category | flops | bytes accessed | tf_op | source)
XLA Modules:
  0.0 287.8 jit_solution(15352802801149326981)
XLA Ops:
  0.6 7.6 %collective-permute-start = (bf16[1,192,256]{2,1,0:T(8,128)(2,1)}, bf16[1,192,256]{2,1,0:T(8,128)(2,1)S(1)}, u32[]{:S(2)}, u32[]{:S(2)}) collective-permute-start(bf16[1,192,256]{2,1,0:T(8,128)(2,1)} %bitcast.95), channel_id=1, source_target_pairs={{0,0},{1,1},{2,2},{3,3},{4,32},{5,33},{6,34},{7,35},{8,64},{9,65},... | collective-permute-start | bytes 294920 | tf_op jit(solution)/shard_map/ppermute | solution.py:218
  8.2 9.7 %collective-permute-done = bf16[1,192,256]{2,1,0:T(8,128)(2,1)S(1)} collective-permute-done((bf16[1,192,256]{2,1,0:T(8,128)(2,1)}, bf16[1,192,256]{2,1,0:T(8,128)(2,1)S(1)}, u32[]{:S(2)}, u32[]{:S(2)}) %collective-permute-start) | collective-permute-done | bytes 98336 | tf_op jit(solution)/shard_map/ppermute | solution.py:218
  17.9 2.2 collective-permute-start.1
  20.1 3.9 %collective-permute-done.1 = bf16[1,192,256]{2,1,0:T(8,128)(2,1)S(1)} collective-permute-done((bf16[1,192,256]{2,1,0:T(8,128)(2,1)S(1)}, bf16[1,192,256]{2,1,0:T(8,128)(2,1)S(1)}, u32[]{:S(2)}, u32[]{:S(2)}) %collective-permute-start.1) | collective-permute-done | bytes 98336 | tf_op jit(solution)/shard_map/ppermute | solution.py:39
  24.2 3.2 %collective-permute-start.6 = (bf16[384,256]{1,0:T(8,128)(2,1)S(1)}, bf16[384,256]{1,0:T(8,128)(2,1)S(1)}, u32[]{:S(2)}, u32[]{:S(2)}) collective-permute-start(bf16[384,256]{1,0:T(8,128)(2,1)S(1)} %maximum_select_fusion.1), channel_id=1, source_target_pairs={{0,28},{4,0},{8,4},{12,8},{16,12},{20,16},{24,20},{28,24},{1,29},{... | collective-permute-start | bytes 589832 | tf_op jit(solution)/shard_map/ppermute | solution.py:39
  28.2 2.9 %collective-permute-done.2 = bf16[384,256]{1,0:T(8,128)(2,1)S(1)} collective-permute-done((bf16[384,256]{1,0:T(8,128)(2,1)S(1)}, bf16[384,256]{1,0:T(8,128)(2,1)S(1)}, u32[]{:S(2)}, u32[]{:S(2)}) %collective-permute-start.2) | collective-permute-done | bytes 196640 | tf_op jit(solution)/shard_map/ppermute | solution.py:39
  31.1 3.2 %collective-permute-start.7 = (bf16[384,256]{1,0:T(8,128)(2,1)S(1)}, bf16[384,256]{1,0:T(8,128)(2,1)S(1)}, u32[]{:S(2)}, u32[]{:S(2)}) collective-permute-start(bf16[384,256]{1,0:T(8,128)(2,1)S(1)} %collective-permute-done.6), channel_id=1, source_target_pairs={{0,28},{4,0},{8,4},{12,8},{16,12},{20,16},{24,20},{28,24},{1,29},{... | collective-permute-start | bytes 589832 | tf_op jit(solution)/shard_map/ppermute | solution.py:39
  35.0 2.9 %collective-permute-done.3 = bf16[384,256]{1,0:T(8,128)(2,1)S(1)} collective-permute-done((bf16[384,256]{1,0:T(8,128)(2,1)S(1)}, bf16[384,256]{1,0:T(8,128)(2,1)S(1)}, u32[]{:S(2)}, u32[]{:S(2)}) %collective-permute-start.3) | collective-permute-done | bytes 196640 | tf_op jit(solution)/shard_map/ppermute | solution.py:39
  38.0 3.3 %collective-permute-start.8 = (bf16[384,256]{1,0:T(8,128)(2,1)S(1)}, bf16[384,256]{1,0:T(8,128)(2,1)S(1)}, u32[]{:S(2)}, u32[]{:S(2)}) collective-permute-start(bf16[384,256]{1,0:T(8,128)(2,1)S(1)} %collective-permute-done.7), channel_id=1, source_target_pairs={{0,28},{4,0},{8,4},{12,8},{16,12},{20,16},{24,20},{28,24},{1,29},{... | collective-permute-start | bytes 589832 | tf_op jit(solution)/shard_map/ppermute | solution.py:39
  42.0 3.9 %collective-permute-done.4 = bf16[384,256]{1,0:T(8,128)(2,1)S(1)} collective-permute-done((bf16[384,256]{1,0:T(8,128)(2,1)S(1)}, bf16[384,256]{1,0:T(8,128)(2,1)S(1)}, u32[]{:S(2)}, u32[]{:S(2)}) %collective-permute-start.4) | collective-permute-done | bytes 196640 | tf_op jit(solution)/shard_map/ppermute | solution.py:39
  46.6 6.2 %collective-permute-done.5 = bf16[384,256]{1,0:T(8,128)(2,1)S(1)} collective-permute-done((bf16[384,256]{1,0:T(8,128)(2,1)S(1)}, bf16[384,256]{1,0:T(8,128)(2,1)S(1)}, u32[]{:S(2)}, u32[]{:S(2)}) %collective-permute-start.5) | collective-permute-done | bytes 196640 | tf_op jit(solution)/shard_map/ppermute | solution.py:39
  56.3 8.9 %all-to-all-start = ((f32[32,8,128]{2,1,0:T(8,128)}), f32[32,8,128]{2,1,0:T(8,128)S(1)}, u32[]{:S(2)}, u32[]{:S(2)}) async-start(f32[32,8,128]{2,1,0:T(8,128)} %broadcast_in_dim.24), calls=%async_computation | async-start | bytes 262144 | tf_op jit(solution)/shard_map/all_to_all | solution.py:53
  65.9 10.1 %all-to-all-done = f32[32,8,128]{2,1,0:T(8,128)S(1)} async-done(((f32[32,8,128]{2,1,0:T(8,128)}), f32[32,8,128]{2,1,0:T(8,128)S(1)}, u32[]{:S(2)}, u32[]{:S(2)}) %all-to-all-start) | async-done | bytes 131104 | tf_op jit(solution)/shard_map/all_to_all | solution.py:53
  77.1 6.6 %all-to-all-start.1 = ((f32[8,16,128]{2,1,0:T(8,128)}), f32[8,16,128]{2,1,0:T(8,128)S(1)}, u32[]{:S(2)}, u32[]{:S(2)}) async-start(f32[8,16,128]{2,1,0:T(8,128)} %broadcast_in_dim.27), calls=%async_computation.1 | async-start | bytes 131072 | tf_op jit(solution)/shard_map/all_to_all | solution.py:53
  84.1 3.2 %all-to-all-done.1 = f32[8,16,128]{2,1,0:T(8,128)S(1)} async-done(((f32[8,16,128]{2,1,0:T(8,128)}), f32[8,16,128]{2,1,0:T(8,128)S(1)}, u32[]{:S(2)}, u32[]{:S(2)}) %all-to-all-start.1) | async-done | bytes 65568 | tf_op jit(solution)/shard_map/all_to_all | solution.py:53
  87.3 7.9 %norm_matmul.1 = (bf16[8,768,256]{2,1,0:T(8,128)(2,1)S(1)}, bf16[8,768,256]{2,1,0:T(8,128)(2,1)S(1)}) custom-call(s32[2]{0:T(128)S(1)} %pad_add_fusion.idx, bf16[8,384,256]{2,1,0:T(8,128)(2,1)} %bitcast_dynamic-update-slice_fusion.own, bf16[8,384,256]{2,1,0:T(8,128)(2,1)} %collective-permute-done.9.other, f32[8,2,256]{2,1,0:T(2,128)S(1)} %squeeze_reshape.3.stats, ...), custom_call_target="tpu_custom_call" | custom-call | flops 2415919104 | bytes 10000000 | tf_op jit(solution)/shard_map/norm_matmul/pallas_call | solution.py:74
  95.2 1.7 copy-done.3
  96.9 1.7 copy-done.4
  98.6 7.2 %all-to-all-start.2 = ((bf16[8,768,256]{2,1,0:T(8,128)(2,1)}), bf16[8,768,256]{2,1,0:T(8,128)(2,1)}, u32[]{:S(2)}, u32[]{:S(2)}) async-start(bf16[8,768,256]{2,1,0:T(8,128)(2,1)} %copy-done.3), calls=%async_computation.2 | async-start | bytes 6291456 | tf_op jit(solution)/shard_map/all_to_all | solution.py:255
  106.0 41.3 %all-to-all-done.2 = bf16[8,768,256]{2,1,0:T(8,128)(2,1)} async-done(((bf16[8,768,256]{2,1,0:T(8,128)(2,1)}), bf16[8,768,256]{2,1,0:T(8,128)(2,1)}, u32[]{:S(2)}, u32[]{:S(2)}) %all-to-all-start.2) | async-done | bytes 3145760 | tf_op jit(solution)/shard_map/all_to_all | solution.py:255
  147.3 2.4 convert_reduce_fusion
  149.7 0.8 fusion
  150.8 40.8 %all_to_all.35.grad.refs_1_ = bf16[8,768,256]{2,1,0:T(8,128)(2,1)S(1)} all-to-all(bf16[8,768,256]{2,1,0:T(8,128)(2,1)S(1)} %broadcast_in_dim.56), channel_id=1, replica_groups=mesh['x'=4,'yl'=2,'z'=8,'yh'=2,'k'=2] {'x','yl'}, dimensions={0} | all-to-all | bytes 6291456 | tf_op jit(solution)/shard_map/all_to_all | solution.py:53
  191.6 5.7 %back_matmul.1 = (bf16[8,384,256]{2,1,0:T(8,128)(2,1)S(1)}, bf16[8,384,256]{2,1,0:T(8,128)(2,1)}) custom-call(s32[2]{0:T(128)S(1)} %pad_add_fusion.idx, bf16[768,768]{1,0:T(8,128)(2,1)S(1)} %copy-done, bf16[8,768,256]{2,1,0:T(8,128)(2,1)S(1)} %all_to_all.35.grad.refs_1_), custom_call_target="tpu_custom_call" | custom-call | flops 2415919104 | bytes 8000000 | tf_op jit(solution)/shard_map/back_matmul/pallas_call | solution.py:108
  197.3 3.7 %collective-permute-done.10 = bf16[8,384,256]{2,1,0:T(8,128)(2,1)} collective-permute-done((bf16[8,384,256]{2,1,0:T(8,128)(2,1)}, bf16[8,384,256]{2,1,0:T(8,128)(2,1)}, u32[]{:S(2)}, u32[]{:S(2)}) %collective-permute-start.10) | collective-permute-done | bytes 1572896 | tf_op jit(solution)/shard_map/ppermute | solution.py:39
  201.1 1.8 fusion.26
  203.9 4.7 %all-to-all-start.4 = ((f32[32,4,128]{2,1,0:T(4,128)}), f32[32,4,128]{2,1,0:T(4,128)}, u32[]{:S(2)}, u32[]{:S(2)}) async-start(f32[32,4,128]{2,1,0:T(4,128)} %broadcast_in_dim.57), calls=%async_computation.4 | async-start | bytes 131072 | tf_op jit(solution)/shard_map/all_to_all | solution.py:53
  208.6 3.1 %collective-permute-start.15 = (bf16[384,256]{1,0:T(8,128)(2,1)}, bf16[384,256]{1,0:T(8,128)(2,1)}, u32[]{:S(2)}, u32[]{:S(2)}) collective-permute-start(bf16[384,256]{1,0:T(8,128)(2,1)} %get-tuple-element.44), channel_id=1, source_target_pairs={{0,28},{4,0},{8,4},{12,8},{16,12},{20,16},{24,20},{28,24},{1,29},{... | collective-permute-start | bytes 589832 | tf_op jit(solution)/shard_map/ppermute | solution.py:39
  211.6 1.7 fusion.18
  213.3 1.9 copy-done.2
  215.2 1.9 copy-done.5
  217.1 6.1 %weight_grads.1 = (f32[768,768]{1,0:T(8,128)}, f32[768,1]{1,0:T(8,128)S(1)}, f32[768,1]{1,0:T(8,128)S(1)}) custom-call(bf16[8,768,256]{2,1,0:T(8,128)(2,1)S(1)} %copy-done.5, bf16[8,768,256]{2,1,0:T(8,128)(2,1)S(1)} %copy-done.2, bf16[768,768]{1,0:T(8,128)(2,1)S(1)} %copy-done), custom_call_target="tpu_custom_call" | custom-call | flops 2415919104 | bytes 10000000 | tf_op jit(solution)/shard_map/weight_grads/pallas_call | solution.py:157
  223.4 2.2 fusion.17
  226.3 2.5 collective-permute-start.16
  229.4 8.7 %all-to-all-start.5 = ((f32[32,8,128]{2,1,0:T(8,128)}), f32[32,8,128]{2,1,0:T(8,128)S(1)}, u32[]{:S(2)}, u32[]{:S(2)}) async-start(f32[32,8,128]{2,1,0:T(8,128)} %broadcast_in_dim.59), calls=%async_computation.5 | async-start | bytes 262144 | tf_op jit(solution)/shard_map/all_to_all | solution.py:53
  238.5 0.9 copy.27
  239.4 0.9 reduce_sum.98
  240.3 8.6 %all-to-all-done.5 = f32[32,8,128]{2,1,0:T(8,128)S(1)} async-done(((f32[32,8,128]{2,1,0:T(8,128)}), f32[32,8,128]{2,1,0:T(8,128)S(1)}, u32[]{:S(2)}, u32[]{:S(2)}) %all-to-all-start.5) | async-done | bytes 131104 | tf_op jit(solution)/shard_map/all_to_all | solution.py:53
  249.6 5.6 %all-to-all-start.6 = ((f32[8,8,128]{2,1,0:T(8,128)}), f32[8,8,128]{2,1,0:T(8,128)S(1)}, u32[]{:S(2)}, u32[]{:S(2)}) async-start(f32[8,8,128]{2,1,0:T(8,128)} %broadcast_in_dim.60), calls=%async_computation.6 | async-start | bytes 65536 | tf_op jit(solution)/shard_map/all_to_all | solution.py:53
  255.2 1.3 fusion.16
  256.5 1.6 collective-permute-start.14
  258.1 1.7 collective-permute-start.17
  259.9 0.8 reduce
  260.7 3.9 %collective-permute-done.14 = bf16[384,256]{1,0:T(8,128)(2,1)S(1)} collective-permute-done((bf16[384,256]{1,0:T(8,128)(2,1)S(1)}, bf16[384,256]{1,0:T(8,128)(2,1)S(1)}, u32[]{:S(2)}, u32[]{:S(2)}) %collective-permute-start.14) | collective-permute-done | bytes 196640 | tf_op jit(solution)/shard_map/ppermute | solution.py:39
  264.6 1.0 bitcast_add_fusion
  266.2 5.7 %collective-permute-done.18 = bf16[192,256]{1,0:T(8,128)(2,1)S(1)} collective-permute-done((bf16[192,256]{1,0:T(8,128)(2,1)S(1)}, bf16[192,256]{1,0:T(8,128)(2,1)S(1)}, u32[]{:S(2)}, u32[]{:S(2)}) %collective-permute-start.18) | collective-permute-done | bytes 98336 | tf_op jit(solution)/shard_map/ppermute | solution.py:39
  271.9 4.7 %collective-permute-start.19 = (bf16[1,192,256]{2,1,0:T(8,128)(2,1)S(1)}, bf16[1,192,256]{2,1,0:T(8,128)(2,1)S(1)}, u32[]{:S(2)}, u32[]{:S(2)}) collective-permute-start(bf16[1,192,256]{2,1,0:T(8,128)(2,1)S(1)} %fusion.30), channel_id=1, source_target_pairs={{0,0},{1,1},{2,2},{3,3},{32,4},{33,5},{34,6},{35,7},{64,8},{65,9},... | collective-permute-start | bytes 294920 | tf_op jit(solution)/shard_map/ppermute | solution.py:273
  277.2 9.9 %collective-permute-done.19 = bf16[1,192,256]{2,1,0:T(8,128)(2,1)S(1)} collective-permute-done((bf16[1,192,256]{2,1,0:T(8,128)(2,1)S(1)}, bf16[1,192,256]{2,1,0:T(8,128)(2,1)S(1)}, u32[]{:S(2)}, u32[]{:S(2)}) %collective-permute-start.19) | collective-permute-done | bytes 98336 | tf_op jit(solution)/shard_map/ppermute | solution.py:273
  (96 shorter events, 14.9 us)
Async XLA Ops:
  0.6 17.3 %collective-permute-start = (bf16[1,192,256]{2,1,0:T(8,128)(2,1)}, bf16[1,192,256]{2,1,0:T(8,128)(2,1)S(1)}, u32[]{:S(2)}, u32[]{:S(2)}) collective-permute-start(bf16[1,192,256]{2,1,0:T(8,128)(2,1)} %bitcast.95), channel_id=1, source_target_pairs={{0,0},{1,1},{2,2},{3,3},{4,32},{5,33},{6,34},{7,35},{8,64},{9,65},... | collective-permute-start | bytes 294920 | tf_op jit(solution)/shard_map/ppermute | solution.py:218
  17.9 6.1 %collective-permute-start.1 = (bf16[1,192,256]{2,1,0:T(8,128)(2,1)S(1)}, bf16[1,192,256]{2,1,0:T(8,128)(2,1)S(1)}, u32[]{:S(2)}, u32[]{:S(2)}) collective-permute-start(bf16[1,192,256]{2,1,0:T(8,128)(2,1)S(1)} %collective-permute-done), channel_id=1, source_target_pairs={{0,2},{2,0},{1,3},{3,1},{4,6},{6,4},{5,7},{7,5},{8,10},{10,8},{9,1... | collective-permute-start | bytes 294920 | tf_op jit(solution)/shard_map/ppermute | solution.py:39
  24.1 31.4 %copy-start.12 = (bf16[192]{0:T(256)(128)(2,1)S(1)}, bf16[192]{0:T(256)(128)(2,1)}, u32[]{:S(2)}) copy-start(bf16[192]{0:T(256)(128)(2,1)} %param.6) | copy-start | bytes 1156
  24.1 31.4 %copy-start.9 = (bf16[256,192]{0,1:T(8,128)(2,1)S(1)}, bf16[256,192]{0,1:T(8,128)(2,1)}, u32[]{:S(2)}) copy-start(bf16[256,192]{0,1:T(8,128)(2,1)} %param.5) | copy-start | bytes 294916
  24.1 7.0 %collective-permute-start.2 = (bf16[384,256]{1,0:T(8,128)(2,1)S(1)}, bf16[384,256]{1,0:T(8,128)(2,1)S(1)}, u32[]{:S(2)}, u32[]{:S(2)}) collective-permute-start(bf16[384,256]{1,0:T(8,128)(2,1)S(1)} %maximum_select_fusion.1), channel_id=1, source_target_pairs={{0,4},{4,8},{8,12},{12,16},{16,20},{20,24},{24,28},{28,0},{1,5},{5... | collective-permute-start | bytes 589832 | tf_op jit(solution)/shard_map/ppermute | solution.py:39
  24.2 6.9 %collective-permute-start.6 = (bf16[384,256]{1,0:T(8,128)(2,1)S(1)}, bf16[384,256]{1,0:T(8,128)(2,1)S(1)}, u32[]{:S(2)}, u32[]{:S(2)}) collective-permute-start(bf16[384,256]{1,0:T(8,128)(2,1)S(1)} %maximum_select_fusion.1), channel_id=1, source_target_pairs={{0,28},{4,0},{8,4},{12,8},{16,12},{20,16},{24,20},{28,24},{1,29},{... | collective-permute-start | bytes 589832 | tf_op jit(solution)/shard_map/ppermute | solution.py:39
  28.2 37.1 %copy-start = (bf16[768,768]{1,0:T(8,128)(2,1)S(1)}, bf16[768,768]{1,0:T(8,128)(2,1)}, u32[]{:S(2)}) copy-start(bf16[768,768]{1,0:T(8,128)(2,1)} %refs_2_.1) | copy-start | bytes 3538948
  31.1 6.9 %collective-permute-start.3 = (bf16[384,256]{1,0:T(8,128)(2,1)S(1)}, bf16[384,256]{1,0:T(8,128)(2,1)S(1)}, u32[]{:S(2)}, u32[]{:S(2)}) collective-permute-start(bf16[384,256]{1,0:T(8,128)(2,1)S(1)} %collective-permute-done.2), channel_id=1, source_target_pairs={{0,4},{4,8},{8,12},{12,16},{16,20},{20,24},{24,28},{28,0},{1,5},{5... | collective-permute-start | bytes 589832 | tf_op jit(solution)/shard_map/ppermute | solution.py:39
  31.1 6.9 %collective-permute-start.7 = (bf16[384,256]{1,0:T(8,128)(2,1)S(1)}, bf16[384,256]{1,0:T(8,128)(2,1)S(1)}, u32[]{:S(2)}, u32[]{:S(2)}) collective-permute-start(bf16[384,256]{1,0:T(8,128)(2,1)S(1)} %collective-permute-done.6), channel_id=1, source_target_pairs={{0,28},{4,0},{8,4},{12,8},{16,12},{20,16},{24,20},{28,24},{1,29},{... | collective-permute-start | bytes 589832 | tf_op jit(solution)/shard_map/ppermute | solution.py:39
  38.0 7.9 %collective-permute-start.4 = (bf16[384,256]{1,0:T(8,128)(2,1)S(1)}, bf16[384,256]{1,0:T(8,128)(2,1)S(1)}, u32[]{:S(2)}, u32[]{:S(2)}) collective-permute-start(bf16[384,256]{1,0:T(8,128)(2,1)S(1)} %collective-permute-done.3), channel_id=1, source_target_pairs={{0,4},{4,8},{8,12},{12,16},{16,20},{20,24},{24,28},{28,0},{1,5},{5... | collective-permute-start | bytes 589832 | tf_op jit(solution)/shard_map/ppermute | solution.py:39
  38.0 15.5 %collective-permute-start.8 = (bf16[384,256]{1,0:T(8,128)(2,1)S(1)}, bf16[384,256]{1,0:T(8,128)(2,1)S(1)}, u32[]{:S(2)}, u32[]{:S(2)}) collective-permute-start(bf16[384,256]{1,0:T(8,128)(2,1)S(1)} %collective-permute-done.7), channel_id=1, source_target_pairs={{0,28},{4,0},{8,4},{12,8},{16,12},{20,16},{24,20},{28,24},{1,29},{... | collective-permute-start | bytes 589832 | tf_op jit(solution)/shard_map/ppermute | solution.py:39
  45.9 6.9 %collective-permute-start.5 = (bf16[384,256]{1,0:T(8,128)(2,1)S(1)}, bf16[384,256]{1,0:T(8,128)(2,1)S(1)}, u32[]{:S(2)}, u32[]{:S(2)}) collective-permute-start(bf16[384,256]{1,0:T(8,128)(2,1)S(1)} %collective-permute-done.4), channel_id=1, source_target_pairs={{0,4},{4,8},{8,12},{12,16},{16,20},{20,24},{24,28},{28,0},{1,5},{5... | collective-permute-start | bytes 589832 | tf_op jit(solution)/shard_map/ppermute | solution.py:39
  55.5 31.8 %collective-permute-start.9 = (bf16[8,384,256]{2,1,0:T(8,128)(2,1)}, bf16[8,384,256]{2,1,0:T(8,128)(2,1)}, u32[]{:S(2)}, u32[]{:S(2)}) collective-permute-start(bf16[8,384,256]{2,1,0:T(8,128)(2,1)} %bitcast_dynamic-update-slice_fusion.own), channel_id=1, source_target_pairs={{0,1},{1,0},{2,3},{3,2},{4,5},{5,4},{6,7},{7,6},{8,9},{9,8},{10,11... | collective-permute-start | bytes 4718600 | tf_op jit(solution)/shard_map/ppermute | solution.py:39
  56.3 19.6 %all-to-all-start = ((f32[32,8,128]{2,1,0:T(8,128)}), f32[32,8,128]{2,1,0:T(8,128)S(1)}, u32[]{:S(2)}, u32[]{:S(2)}) async-start(f32[32,8,128]{2,1,0:T(8,128)} %broadcast_in_dim.24), calls=%async_computation | async-start | bytes 262144 | tf_op jit(solution)/shard_map/all_to_all | solution.py:53
  77.1 10.1 %all-to-all-start.1 = ((f32[8,16,128]{2,1,0:T(8,128)}), f32[8,16,128]{2,1,0:T(8,128)S(1)}, u32[]{:S(2)}, u32[]{:S(2)}) async-start(f32[8,16,128]{2,1,0:T(8,128)} %broadcast_in_dim.27), calls=%async_computation.1 | async-start | bytes 131072 | tf_op jit(solution)/shard_map/all_to_all | solution.py:53
  95.2 1.7 copy-start.3
  96.9 1.7 copy-start.4
  98.6 7.2 %copy-start.8 = (bf16[256,768]{1,0:T(8,128)(2,1)S(1)}, bf16[256,768]{1,0:T(8,128)(2,1)}, u32[]{:S(2)}) copy-start(bf16[256,768]{1,0:T(8,128)(2,1)} %param.9) | copy-start | bytes 1179652
  98.6 48.7 %all-to-all-start.2 = ((bf16[8,768,256]{2,1,0:T(8,128)(2,1)}), bf16[8,768,256]{2,1,0:T(8,128)(2,1)}, u32[]{:S(2)}, u32[]{:S(2)}) async-start(bf16[8,768,256]{2,1,0:T(8,128)(2,1)} %copy-done.3), calls=%async_computation.2 | async-start | bytes 6291456 | tf_op jit(solution)/shard_map/all_to_all | solution.py:255
  106.0 43.7 %copy-start.11 = (f32[768]{0:T(1024)S(1)}, f32[768]{0:T(1024)}, u32[]{:S(2)}) copy-start(f32[768]{0:T(1024)} %param.8) | copy-start | bytes 9220
  149.7 1.0 copy-start.6
  191.6 5.7 %copy-start.1 = (bf16[8,768,256]{2,1,0:T(8,128)(2,1)}, bf16[8,768,256]{2,1,0:T(8,128)(2,1)S(1)}, u32[]{:S(2)}) copy-start(bf16[8,768,256]{2,1,0:T(8,128)(2,1)S(1)} %all_to_all.35.grad.refs_1_) | copy-start | bytes 9437188
  197.3 3.8 %collective-permute-start.10 = (bf16[8,384,256]{2,1,0:T(8,128)(2,1)}, bf16[8,384,256]{2,1,0:T(8,128)(2,1)}, u32[]{:S(2)}, u32[]{:S(2)}) collective-permute-start(bf16[8,384,256]{2,1,0:T(8,128)(2,1)} %get-tuple-element.14), channel_id=1, source_target_pairs={{0,1},{1,0},{2,3},{3,2},{4,5},{5,4},{6,7},{7,6},{8,9},{9,8},{10,11... | collective-permute-start | bytes 4718600 | tf_op jit(solution)/shard_map/ppermute | solution.py:39
  202.9 8.8 %collective-permute-start.11 = (bf16[384,256]{1,0:T(8,128)(2,1)S(1)}, bf16[384,256]{1,0:T(8,128)(2,1)S(1)}, u32[]{:S(2)}, u32[]{:S(2)}) collective-permute-start(bf16[384,256]{1,0:T(8,128)(2,1)S(1)} %get-tuple-element.43), channel_id=1, source_target_pairs={{0,4},{4,8},{8,12},{12,16},{16,20},{20,24},{24,28},{28,0},{1,5},{5... | collective-permute-start | bytes 589832 | tf_op jit(solution)/shard_map/ppermute | solution.py:39
  203.9 24.9 %all-to-all-start.4 = ((f32[32,4,128]{2,1,0:T(4,128)}), f32[32,4,128]{2,1,0:T(4,128)}, u32[]{:S(2)}, u32[]{:S(2)}) async-start(f32[32,4,128]{2,1,0:T(4,128)} %broadcast_in_dim.57), calls=%async_computation.4 | async-start | bytes 131072 | tf_op jit(solution)/shard_map/all_to_all | solution.py:53
  208.6 14.8 %collective-permute-start.15 = (bf16[384,256]{1,0:T(8,128)(2,1)}, bf16[384,256]{1,0:T(8,128)(2,1)}, u32[]{:S(2)}, u32[]{:S(2)}) collective-permute-start(bf16[384,256]{1,0:T(8,128)(2,1)} %get-tuple-element.44), channel_id=1, source_target_pairs={{0,28},{4,0},{8,4},{12,8},{16,12},{20,16},{24,20},{28,24},{1,29},{... | collective-permute-start | bytes 589832 | tf_op jit(solution)/shard_map/ppermute | solution.py:39
  213.3 10.0 %collective-permute-start.12 = (bf16[384,256]{1,0:T(8,128)(2,1)}, bf16[384,256]{1,0:T(8,128)(2,1)}, u32[]{:S(2)}, u32[]{:S(2)}) collective-permute-start(bf16[384,256]{1,0:T(8,128)(2,1)} %fusion.18), channel_id=1, source_target_pairs={{0,4},{4,8},{8,12},{12,16},{16,20},{20,24},{24,28},{28,0},{1,5},{5... | collective-permute-start | bytes 589832 | tf_op jit(solution)/shard_map/ppermute | solution.py:39
  213.3 1.9 copy-start.2
  215.2 1.9 copy-start.5
  223.2 15.0 %copy-start.7 = (f32[768,256]{1,0:T(8,128)S(1)}, f32[768,256]{1,0:T(8,128)}, u32[]{:S(2)}) copy-start(f32[768,256]{1,0:T(8,128)} %copy-done.6) | copy-start | bytes 2359300
  225.5 29.7 %collective-permute-start.13 = (bf16[384,256]{1,0:T(8,128)(2,1)}, bf16[384,256]{1,0:T(8,128)(2,1)S(1)}, u32[]{:S(2)}, u32[]{:S(2)}) collective-permute-start(bf16[384,256]{1,0:T(8,128)(2,1)} %get-tuple-element.41), channel_id=1, source_target_pairs={{0,4},{4,8},{8,12},{12,16},{16,20},{20,24},{24,28},{28,0},{1,5},{5... | collective-permute-start | bytes 589832 | tf_op jit(solution)/shard_map/ppermute | solution.py:39
  226.3 29.0 %collective-permute-start.16 = (bf16[384,256]{1,0:T(8,128)(2,1)}, bf16[384,256]{1,0:T(8,128)(2,1)}, u32[]{:S(2)}, u32[]{:S(2)}) collective-permute-start(bf16[384,256]{1,0:T(8,128)(2,1)} %get-tuple-element.42), channel_id=1, source_target_pairs={{0,28},{4,0},{8,4},{12,8},{16,12},{20,16},{24,20},{28,24},{1,29},{... | collective-permute-start | bytes 589832 | tf_op jit(solution)/shard_map/ppermute | solution.py:39
  229.4 19.5 %all-to-all-start.5 = ((f32[32,8,128]{2,1,0:T(8,128)}), f32[32,8,128]{2,1,0:T(8,128)S(1)}, u32[]{:S(2)}, u32[]{:S(2)}) async-start(f32[32,8,128]{2,1,0:T(8,128)} %broadcast_in_dim.59), calls=%async_computation.5 | async-start | bytes 262144 | tf_op jit(solution)/shard_map/all_to_all | solution.py:53
  249.6 11.0 %all-to-all-start.6 = ((f32[8,8,128]{2,1,0:T(8,128)}), f32[8,8,128]{2,1,0:T(8,128)S(1)}, u32[]{:S(2)}, u32[]{:S(2)}) async-start(f32[8,8,128]{2,1,0:T(8,128)} %broadcast_in_dim.60), calls=%async_computation.6 | async-start | bytes 65536 | tf_op jit(solution)/shard_map/all_to_all | solution.py:53
  256.5 20.1 %copy-start.13 = (bf16[192]{0:T(256)(128)(2,1)S(1)}, bf16[192]{0:T(256)(128)(2,1)}, u32[]{:S(2)}) copy-start(bf16[192]{0:T(256)(128)(2,1)} %param.6) | copy-start | bytes 1156
  256.5 30.5 %copy-start.10 = (bf16[256,192]{0,1:T(8,128)(2,1)S(1)}, bf16[256,192]{0,1:T(8,128)(2,1)}, u32[]{:S(2)}) copy-start(bf16[256,192]{0,1:T(8,128)(2,1)} %param.5) | copy-start | bytes 294916
  256.5 8.1 %collective-permute-start.14 = (bf16[384,256]{1,0:T(8,128)(2,1)S(1)}, bf16[384,256]{1,0:T(8,128)(2,1)S(1)}, u32[]{:S(2)}, u32[]{:S(2)}) collective-permute-start(bf16[384,256]{1,0:T(8,128)(2,1)S(1)} %get-tuple-element.39), channel_id=1, source_target_pairs={{0,4},{4,8},{8,12},{12,16},{16,20},{20,24},{24,28},{28,0},{1,5},{5... | collective-permute-start | bytes 589832 | tf_op jit(solution)/shard_map/ppermute | solution.py:39
  258.1 6.5 %collective-permute-start.17 = (bf16[384,256]{1,0:T(8,128)(2,1)S(1)}, bf16[384,256]{1,0:T(8,128)(2,1)S(1)}, u32[]{:S(2)}, u32[]{:S(2)}) collective-permute-start(bf16[384,256]{1,0:T(8,128)(2,1)S(1)} %get-tuple-element.40), channel_id=1, source_target_pairs={{0,28},{4,0},{8,4},{12,8},{16,12},{20,16},{24,20},{28,24},{1,29},{... | collective-permute-start | bytes 589832 | tf_op jit(solution)/shard_map/ppermute | solution.py:39
  265.7 6.2 %collective-permute-start.18 = (bf16[192,256]{1,0:T(8,128)(2,1)S(1)}, bf16[192,256]{1,0:T(8,128)(2,1)S(1)}, u32[]{:S(2)}, u32[]{:S(2)}) collective-permute-start(bf16[192,256]{1,0:T(8,128)(2,1)S(1)} %select_convert_fusion), channel_id=1, source_target_pairs={{0,2},{2,0},{1,3},{3,1},{4,6},{6,4},{5,7},{7,5},{8,10},{10,8},{9,1... | collective-permute-start | bytes 294920 | tf_op jit(solution)/shard_map/ppermute | solution.py:39
  271.9 15.1 %collective-permute-start.19 = (bf16[1,192,256]{2,1,0:T(8,128)(2,1)S(1)}, bf16[1,192,256]{2,1,0:T(8,128)(2,1)S(1)}, u32[]{:S(2)}, u32[]{:S(2)}) collective-permute-start(bf16[1,192,256]{2,1,0:T(8,128)(2,1)S(1)} %fusion.30), channel_id=1, source_target_pairs={{0,0},{1,1},{2,2},{3,3},{32,4},{33,5},{34,6},{35,7},{64,8},{65,9},... | collective-permute-start | bytes 294920 | tf_op jit(solution)/shard_map/ppermute | solution.py:273

commit v2 on v0

v2 whole, which is shorter than its diff:
```python
import math

import jax
import jax.numpy as jnp
from jax import lax
from jax.experimental import pallas as pl
from jax.experimental.pallas import tpu as pltpu
from jax.sharding import Mesh
from jax.sharding import PartitionSpec as P

D = 6144
PANEL = 768
BLOCK = 192
TOK = 256
Q = 64
VMEM = 60 * 2**20
AXES = ("x", "yl", "z", "yh", "k")
SIZES = (4, 2, 8, 2, 2)
ROW = ("x", "yl")
COL = ("z", "yh", "k")
QUAD = ("yh", "k")
f32, bf16 = jnp.float32, jnp.bfloat16


def gelu_parts(preact):
    coeff = math.sqrt(2.0 / math.pi)
    inner = coeff * (preact + 0.044715 * preact * preact * preact)
    tanh_val = jnp.tanh(inner)
    value = 0.5 * preact * (1.0 + tanh_val)
    slope = 0.5 * (1.0 + tanh_val) + 0.5 * preact * (1.0 - tanh_val * tanh_val) * coeff * (
        1.0 + 3.0 * 0.044715 * preact * preact
    )
    return (value, slope)


def shift(value, axis, by):
    size = SIZES[AXES.index(axis)]
    return lax.ppermute(value, axis, [(i, (i + by) % size) for i in range(size)])


def swap(value, m):
    return lax.ppermute(value, QUAD, [(i, i ^ m) for i in range(4)]) if m else value


def transpose(value):
    pairs = []
    for r in range(8):
        for z in range(8):
            for q in range(4):
                pairs.append((r * 32 + z * 4 + q, z * 32 + r * 4 + q))
    return lax.ppermute(value, AXES, pairs)


def to_all(value, axes, count):
    return lax.all_to_all(
        jnp.broadcast_to(value[None], (count,) + value.shape), axes, 0, 0
    )


def pick(stack, index):
    return lax.dynamic_index_in_dim(stack, index, 0, keepdims=False)


def trade(stack, q):
    got = jnp.stack([swap(pick(stack, q ^ m), m) for m in range(4)])
    return [pick(got, q ^ i) for i in range(4)]


def in_three(value):
    high = lax.reduce_precision(value, 8, 7)
    middle = lax.reduce_precision(value - high, 8, 7)
    return jnp.concatenate([high, middle, value - high - middle]).astype(bf16)


def padded(rows, count=16):
    return jnp.concatenate([rows, jnp.zeros((count - rows.shape[0], rows.shape[1]), rows.dtype)])


def split(value, count):
    parts = []
    for _ in range(count):
        parts.append(value.astype(bf16).astype(f32))
        value = value - parts[-1]
    return parts


def call(kernel, name, arrays, out_shape, flops):
    vmem = pl.BlockSpec(memory_space=pltpu.VMEM)
    return pl.pallas_call(
        kernel,
        in_specs=[vmem] * len(arrays),
        out_specs=[vmem] * len(out_shape),
        out_shape=out_shape,
        compiler_params=pltpu.CompilerParams(vmem_limit_bytes=VMEM),
        cost_estimate=pl.CostEstimate(flops=flops, bytes_accessed=2**20, transcendentals=0),
        name=name,
    )(*arrays)


def streamed(kernel, name, scalars, blocked, streams, out_shape, scratch):
    vmem = pl.BlockSpec(memory_space=pltpu.VMEM)
    return pl.pallas_call(
        kernel,
        in_specs=[pl.BlockSpec(memory_space=pltpu.SMEM)]
        + [vmem] * len(blocked)
        + [pl.BlockSpec(memory_space=pl.ANY)] * len(streams),
        out_specs=[vmem] * len(out_shape),
        out_shape=out_shape,
        scratch_shapes=scratch + [pltpu.SemaphoreType.DMA((len(streams),))],
        compiler_params=pltpu.CompilerParams(vmem_limit_bytes=VMEM),
        cost_estimate=pl.CostEstimate(flops=0, bytes_accessed=2**20, transcendentals=0),
        name=name,
    )(scalars, *blocked, *streams)


W_SCRATCH = pltpu.VMEM((4, PANEL, PANEL), bf16)
G_SCRATCH = pltpu.VMEM((8 * Q, 4 * PANEL), bf16)


def row_copies(s, rows, all_rows, sems):
    copies = []
    for i in range(8):
        at = pl.ds(pl.multiple_of(s[i] * Q, Q), Q)
        copies.append(pltpu.make_async_copy(rows[i], all_rows.at[at], sems.at[i]))
    return copies


def forward_kernel(s, normed, gain, w0, w1, w2, w3, out, held, sems):
    copies = [
        pltpu.make_async_copy(w, held.at[i], sems.at[i]) for i, w in enumerate((w0, w1, w2, w3))
    ]
    for copy in copies:
        copy.start()
    sums = []
    for i in range(4):
        copies[i].wait()
        w = held[i]
        part = jnp.dot(normed[...], w, preferred_element_type=f32).astype(bf16)
        for j in range(8):
            out[j, :, i * PANEL : (i + 1) * PANEL] = part[j * Q : (j + 1) * Q]
        one = jnp.sum(w.astype(f32) * gain[...], axis=0, keepdims=True)
        sums += [one[:, j * 128 : (j + 1) * 128] for j in range(6)]
    extra = split(jnp.concatenate(sums, axis=0), 2) + [jnp.zeros((16, 128), f32)]
    extra = jnp.concatenate(extra, axis=0).astype(bf16)
    for j in range(8):
        out[j, :, 4 * PANEL :] = extra


def forward(scalars, normed, gain, ws):
    shape = jax.ShapeDtypeStruct((8, Q, 4 * PANEL + 128), bf16)
    return streamed(
        forward_kernel, "forward", scalars, [normed, gain], ws, [shape], [W_SCRATCH]
    )[0]


def backward_kernel(s, normed, pair, *refs):
    rows, ws, (out, held, grads, sems) = refs[:8], refs[8:12], refs[12:]
    copies = row_copies(s, rows, grads, sems)
    for i, w in enumerate(ws):
        copies.append(pltpu.make_async_copy(w, held.at[i], sems.at[8 + i]))
    for copy in copies:
        copy.start()
    for copy in copies[:8]:
        copy.wait()
    total = None
    for i in range(4):
        copies[8 + i].wait()
        part = lax.dot_general(
            grads[:, i * PANEL : (i + 1) * PANEL], held[i], (((1,), (1,)), ((), ())),
            preferred_element_type=f32,
        )
        total = part if total is None else total + part
    sums = jnp.sum(total * normed[...].astype(f32), axis=0, keepdims=True)
    extra = [pair[...]] + split(sums, 3) + [jnp.zeros((12, PANEL), f32)]
    extra = jnp.concatenate(extra, axis=0).astype(bf16)
    total = total.astype(bf16)
    for j in range(8):
        out[j, :Q] = total[j * Q : (j + 1) * Q]
        out[j, Q:] = extra


def backward(scalars, grads, normed, pair, ws):
    shape = jax.ShapeDtypeStruct((8, Q + 16, PANEL), bf16)
    return streamed(
        backward_kernel, "backward", scalars, [normed, pair], [*grads, *ws], [shape],
        [W_SCRATCH, G_SCRATCH],
    )[0]


def weight_kernel(s, normed, *refs):
    rows, (near, near_far, far, own, bias, grads, sems) = refs[:8], refs[8:]
    copies = row_copies(s, rows, grads, sems)
    for copy in copies:
        copy.start()
    for copy in copies:
        copy.wait()
    for i, out in ((3, near_far), (1, far), (2, near), (0, own)):
        at = slice(i * PANEL, (i + 1) * PANEL)
        out[...] = lax.dot_general(
            normed[...], grads[:, at], (((0,), (0,)), ((), ())), preferred_element_type=f32
        ).astype(out.dtype)
    bias[...] = jnp.sum(grads[...].astype(f32), axis=0, keepdims=True)


def weight_products(scalars, normed, grads):
    shapes = [
        jax.ShapeDtypeStruct((PANEL, PANEL), bf16),
        jax.ShapeDtypeStruct((PANEL, PANEL), bf16),
        jax.ShapeDtypeStruct((PANEL, PANEL), f32),
        jax.ShapeDtypeStruct((PANEL, PANEL), f32),
        jax.ShapeDtypeStruct((1, 4 * PANEL), f32),
    ]
    return streamed(
        weight_kernel, "weight_products", scalars, [normed], grads, shapes, [G_SCRATCH]
    )


def collect_kernel(parts, out, pair):
    total = parts[0].astype(f32)
    for j in range(1, 8):
        total = total + parts[j].astype(f32)
    out[:Q] = total[:Q].astype(bf16)
    pair[...] = total[Q : Q + 1]
    rows = jnp.sum(total[Q + 1 : Q + 4], axis=0, keepdims=True)
    extra = split(rows, 3) + [jnp.zeros((13, PANEL), f32)]
    out[Q:] = jnp.concatenate(extra, axis=0).astype(bf16)


def collect(parts):
    shapes = [
        jax.ShapeDtypeStruct((Q + 16, PANEL), bf16),
        jax.ShapeDtypeStruct((1, PANEL), f32),
    ]
    return call(collect_kernel, "collect", [parts], shapes, 0)


def together(*values):
    return lax.optimization_barrier(values)


def per_device(activations, norm_gain, in_weight, in_bias, out_cotangent):
    row = lax.axis_index(ROW)
    z = lax.axis_index("z")
    q = lax.axis_index(QUAD)
    order = (0, 2, 1, 3)
    px, py = lax.axis_index("x"), lax.axis_index("yl")
    around = ((0, 0), (0, 1), (3, 0), (1, 0), (3, 1), (1, 1), (2, 0), (2, 1))
    scalars = jnp.stack([(px + a) % 4 * 2 + (py + b) % 2 for a, b in around]).astype(jnp.int32)

    x = jnp.concatenate(trade(activations.reshape(4, Q, BLOCK), q), axis=1)

    wide = activations.astype(f32)
    small = jnp.concatenate(
        [
            jnp.sum(wide, axis=1),
            jnp.sum(wide * wide, axis=1),
            norm_gain.astype(f32),
            jnp.zeros((64,), f32),
            in_bias,
            jnp.zeros((512,), f32),
        ]
    ).reshape(16, 128)
    smalls = to_all(small, COL, 32).reshape(32, 2048)
    x, smalls = together(x, smalls)
    sums = jnp.sum(smalls[:, : 2 * TOK], axis=0).reshape(2, 4, Q, 1)
    sums = lax.dynamic_index_in_dim(sums, q, 1, keepdims=False)
    gains = smalls[:, 512:704]
    gain = lax.dynamic_slice(gains, (4 * z, 0), (4, BLOCK)).reshape(1, PANEL)
    average = sums[0] / D
    variance = sums[1] / D - average * average
    inv_std = lax.rsqrt(variance + 1e-06)
    x_hat = (x.astype(f32) - average) * inv_std
    normed = (x_hat * gain).astype(bf16)

    normed, weight = together(normed, in_weight)
    normed = transpose(normed)
    w_far, w_near = swap(weight, 2), swap(weight, 1)
    w_far = together(w_far, normed)[0]
    normed = to_all(normed, "z", 8).reshape(8 * Q, PANEL)
    ws = (weight, w_far, w_near, swap(w_far, 1))
    gain_row = lax.dynamic_slice(gains, (4 * row, 0), (4, BLOCK)).reshape(PANEL, 1)
    cot = out_cotangent.reshape(4, Q, PANEL)
    cot = jnp.concatenate([swap(pick(cot, q ^ m), m) for m in order], axis=1)
    normed, ws, gain_row, cot = together(normed, ws, gain_row, cot)

    recv = lax.all_to_all(forward(scalars, normed, gain_row, ws), ROW, 0, 0)
    biases = smalls[:, 768:1536]
    bias = jnp.concatenate([pick(biases, z * 4 + (q ^ m)) for m in order])
    recv, bias = together(recv, bias)
    total = jnp.sum(recv.astype(f32), axis=0)
    linear = total[:, : 4 * PANEL]
    value, slope = gelu_parts(linear + bias)
    hidden = value.astype(bf16)
    grad = (cot.astype(f32) * slope).astype(bf16)

    beside, below, above = shift(grad, "yl", 1), shift(grad, "x", 1), shift(grad, "x", -1)
    below_beside, above_beside = shift(beside, "x", 1), shift(above, "yl", 1)
    across = jnp.concatenate(
        [shift(below[: Q // 2], "x", 1), shift(above[Q // 2 :], "x", -1)], axis=0
    )
    across_beside = shift(across, "yl", 1)
    grads = [grad, beside, below, above, below_beside, above_beside, across, across_beside]
    wsum = (total[:24, 4 * PANEL :] + total[24:48, 4 * PANEL :]).reshape(1, 4 * PANEL)
    pair = jnp.concatenate(
        [jnp.sum(grad.astype(f32) * wsum, axis=1), jnp.sum(grad.astype(f32) * linear, axis=1)]
    )
    hidden, grads = together(hidden, grads)
    got = [swap(hidden[:, i * PANEL : (i + 1) * PANEL], m) for i, m in enumerate(order)]
    got = jnp.stack([got[order.index(m)] for m in range(4)])
    hidden = jnp.concatenate([pick(got, q ^ i) for i in range(4)], axis=0)
    pair = in_three(pair[None]).astype(f32).reshape(1, 384)
    pair = jnp.pad(pair, ((0, 0), (0, 384)))
    grads, pair = together(grads, pair)

    back = backward(scalars, grads, normed, pair, ws)
    back, grads, hidden = together(back, grads, hidden)
    back = lax.all_to_all(back, "z", 0, 0)
    near, near_far, far, own, bias_total = weight_products(scalars, normed, grads)
    near_far = swap(near_far, 1)
    far = (far + near_far.astype(f32)).astype(bf16)
    far = swap(far, 2)

    near = swap(near, 1)
    back, far = together(back, far)
    back, pair = collect(back)
    pair = pair[0, :384].reshape(3, 2, Q, 1)
    pair = pair[0] + pair[1] + pair[2]
    back = transpose(back)
    scaled = back[:Q].astype(f32) * gain
    input_grad = (inv_std * (scaled - pair[0] / D - x_hat * (pair[1] / D))).astype(bf16)
    input_grad = jnp.concatenate([input_grad, back[Q:]])
    input_grad = jnp.stack([input_grad[:, i * BLOCK : (i + 1) * BLOCK] for i in range(4)])
    pieces = trade(input_grad, q)
    bias_total = together(bias_total, input_grad)[0]
    bias_near = bias_total[:, : 2 * PANEL] + swap(bias_total[:, 2 * PANEL :], 1)
    bias_far = swap(bias_near[:, PANEL:], 2)
    input_grad = jnp.concatenate([p[:Q] for p in pieces], axis=0)
    rows = jnp.sum(sum(p[Q : Q + 3].astype(f32) for p in pieces), axis=0)
    gain_grad = rows / norm_gain.astype(f32)

    weight_grad = own + near.astype(f32) + far.astype(f32)
    bias_grad = (bias_near[:, :PANEL] + bias_far)[0]
    return (hidden, input_grad, weight_grad, bias_grad, gain_grad)


def solution(mesh):
    fine = Mesh(mesh.devices.reshape(SIZES), AXES)
    both = P(ROW, COL)
    return jax.shard_map(
        per_device,
        mesh=fine,
        in_specs=(both, P(COL), both, P(COL), both),
        out_specs=(both, both, both, P(COL), P(COL)),
        check_vma=False,
    )
```

time: 592 us -> 260 us (0.44)
  waiting for transfers between devices: 380 us -> 136 us
  blocking collectives: 155 us -> 0 us
  starting transfers between devices: 7.59 us -> 68.5 us
  Pallas kernels: 0 us -> 26.1 us
  matrix products: 22.5 us -> 0 us
  between operations: 13.8 us -> 1.16 us
  other arithmetic: 5.93 us -> 14.9 us
  local copies, waits for them, and re-layouts: 4.12 us -> 10.7 us
    all_gather x3 -> x0, waiting for transfers between devices: 266 us -> none  [the longest x1 189 us: per_device(): lax.all_gather(in_weight, 'row', axis=0, tiled=True)]
    psum x3 -> x0, blocking collectives: 155 us -> none  [the longest x1 72 us: per_device(): lax.psum((jnp.sum(widened, axis=1), jnp.sum(widened * widened, axis=1)),...]
    reduce_scatter x1 -> x0, waiting for transfers between devices: 113 us -> none  [per_device(): lax.psum_scatter(partial_grad.astype(jnp.bfloat16), 'col', scatter_dimens...]
    all_to_all x1 -> x4, waiting for transfers between devices: 0.01 us -> 69.5 us  [the longest x1 43.5 us: per_device(): recv = lax.all_to_all(forward(scalars, normed, gain_row, ws), ROW, 0, 0)]
    ppermute x0 -> x30, waiting for transfers between devices: none -> 66.2 us  [the longest x20 25.9 us: swap(): lax.ppermute(value, QUAD, [(i, i ^ m) for i in range(4)])]
    ppermute x0 -> x30, starting transfers between devices: none -> 43.4 us  [the longest x20 19.7 us: swap(): lax.ppermute(value, QUAD, [(i, i ^ m) for i in range(4)])]
    pallas_call x0 -> x4, Pallas kernels: none -> 26.1 us  [the longest x3 24.1 us: streamed(): pl.pallas_call(kernel, in_specs=[pl.BlockSpec(memory_space=pltpu.SMEM)] +...]
    dot_general x3 -> x0, matrix products: 22.5 us -> none  [the longest x1 8.44 us: per_device(): jnp.dot(normed_full, lax.all_gather(in_weight, 'row', axis=0, tiled=True)...]
  transfers between devices with their start and end apart: 5 -> 34, of which waited for: 3 -> 19; matrix products, arithmetic and copies ran while one was open for 1% -> 7% of each run, Pallas kernels for 0% -> 4%
where the time goes in v2:
time: 260 us; the launch traced here: 257 us
  waiting for transfers between devices  136 us (52%)
  starting transfers between devices  68.5 us (26%)
  Pallas kernels  26.1 us (10%)
  other arithmetic  14.9 us (6%)
  local copies, waits for them, and re-layouts  10.7 us (4%)
    all_to_all x1, waiting for transfers between devices, per_device(): recv = lax.all_to_all(forward(scalars, normed, gain_row, ws), ROW, 0, 0)  43.5 us
    ppermute x20, waiting for transfers between devices, swap(): lax.ppermute(value, QUAD, [(i, i ^ m) for i in range(4)])  25.9 us
    pallas_call x3, Pallas kernels, streamed(): pl.pallas_call(kernel, in_specs=[pl.BlockSpec(memory_space=pltpu.SMEM)] +...  24.1 us
    ppermute x2, waiting for transfers between devices, transpose(): return lax.ppermute(value, AXES, pairs)  23.5 us
    all_to_all x1, waiting for transfers between devices, per_device(): back = lax.all_to_all(back, 'z', 0, 0)  23 us
    ppermute x20, starting transfers between devices, swap(): lax.ppermute(value, QUAD, [(i, i ^ m) for i in range(4)])  19.7 us
    ppermute x8, waiting for transfers between devices, shift(): lax.ppermute(value, axis, [(i, (i + by) % size) for i in range(size)])  16.9 us
    all_to_all x2, starting transfers between devices, to_all(): lax.all_to_all(jnp.broadcast_to(value[None], (count,) + value.shape), axe...  14.1 us
  transfers between devices with their start and end apart: 34, of which 19 were waited for; matrix products, arithmetic and copies ran while one was open for 7% of the time, Pallas kernels for 4%

profile of v2, /device:TPU:14, one launch (start us, length us, event | category | flops | bytes accessed | tf_op | source)
XLA Modules:
  0.0 257.1 jit_solution(14221105616838590510)
XLA Ops:
  0.6 1.0 fusion.9
  1.7 1.4 concatenate.60
  3.8 10.6 %all-to-all-start = ((f32[32,16,128]{2,1,0:T(8,128)}), f32[32,16,128]{2,1,0:T(8,128)S(1)}, u32[]{:S(2)}, u32[]{:S(2)}) async-start(f32[32,16,128]{2,1,0:T(8,128)} %broadcast_in_dim.24), calls=%async_computation | async-start | bytes 524288 | tf_op jit(solution)/shard_map/all_to_all | solution.py:55
  15.5 3.1 %collective-permute-start.2 = (bf16[64,192]{1,0:T(8,128)(2,1)S(1)}, bf16[64,192]{1,0:T(8,128)(2,1)S(1)}, u32[]{:S(2)}, u32[]{:S(2)}) collective-permute-start(bf16[64,192]{1,0:T(8,128)(2,1)S(1)} %get-tuple-element.156), channel_id=1, source_target_pairs={{0,3},{1,2},{2,1},{3,0},{4,7},{5,6},{6,5},{7,4},{8,11},{9,10},{10,... | collective-permute-start | bytes 73736 | tf_op jit(solution)/shard_map/ppermute | solution.py:42
  19.0 1.5 collective-permute-done.2
  20.5 4.1 %collective-permute-done.1 = bf16[64,192]{1,0:T(8,128)(2,1)S(1)} collective-permute-done((bf16[64,192]{1,0:T(8,128)(2,1)S(1)}, bf16[64,192]{1,0:T(8,128)(2,1)S(1)}, u32[]{:S(2)}, u32[]{:S(2)}) %collective-permute-start.1) | collective-permute-done | bytes 24608 | tf_op jit(solution)/shard_map/ppermute | solution.py:42
  24.8 2.7 %all-to-all-done = f32[32,16,128]{2,1,0:T(8,128)S(1)} async-done(((f32[32,16,128]{2,1,0:T(8,128)}), f32[32,16,128]{2,1,0:T(8,128)S(1)}, u32[]{:S(2)}, u32[]{:S(2)}) %all-to-all-start) | async-done | bytes 262176 | tf_op jit(solution)/shard_map/all_to_all | solution.py:55
  28.0 2.4 collective-permute-start.4
  30.4 1.9 collective-permute-start.3
  32.3 14.3 %collective-permute-done.3 = bf16[64,768]{1,0:T(8,128)(2,1)S(1)} collective-permute-done((bf16[64,768]{1,0:T(8,128)(2,1)S(1)}, bf16[64,768]{1,0:T(8,128)(2,1)S(1)}, u32[]{:S(2)}, u32[]{:S(2)}) %collective-permute-start.3) | collective-permute-done | bytes 98336 | tf_op jit(solution)/shard_map/ppermute | solution.py:51
  47.5 3.5 %all-to-all-start.1 = ((bf16[8,64,768]{2,1,0:T(8,128)(2,1)}), bf16[8,64,768]{2,1,0:T(8,128)(2,1)S(1)}, u32[]{:S(2)}, u32[]{:S(2)}) async-start(bf16[8,64,768]{2,1,0:T(8,128)(2,1)} %broadcast_in_dim.25), calls=%async_computation.1 | async-start | bytes 1572864 | tf_op jit(solution)/shard_map/all_to_all | solution.py:55
  51.2 6.4 %collective-permute-done.4.w1.refs_9_ = bf16[768,768]{1,0:T(8,128)(2,1)S(1)} collective-permute-done((bf16[768,768]{1,0:T(8,128)(2,1)S(1)}, bf16[768,768]{1,0:T(8,128)(2,1)S(1)}, u32[]{:S(2)}, u32[]{:S(2)}) %collective-permute-start.4) | collective-permute-done | bytes 1179680 | tf_op jit(solution)/shard_map/ppermute | solution.py:42
  57.6 2.2 dynamic-slice_bitcast_fusion.7
  59.7 1.2 collective-permute-start.9
  61.3 2.0 collective-permute-start.7
  64.0 2.3 collective-permute-done.9
  66.3 2.5 collective-permute-done.7
  68.8 1.7 pad_maximum_fusion
  70.9 1.0 copy.16.gain
  71.9 8.4 %forward.1 = bf16[8,64,3200]{2,1,0:T(8,128)(2,1)} custom-call(s32[8]{0:T(128)} %stack.91.s, bf16[512,768]{1,0:T(8,128)(2,1)} %bitcast.103, f32[768,1]{1,0:T(8,128)} %copy.16.gain, bf16[768,768]{1,0:T(8,128)(2,1)} %refs_8_, bf16[768,768]{1,0:T(8,128)(2,1)} %copy-done.2, bf16[768,768]{1,0:T(8,128)(2,1)} %collective-permute-done.5.w2.refs_10_, ...), custom_call_target="tpu_custom_call" | custom-call | bytes 1048576 | tf_op jit(solution)/shard_map/forward/pallas_call | solution.py:102
  80.3 7.4 %all-to-all-start.2 = ((bf16[8,64,3200]{2,1,0:T(8,128)(2,1)}), bf16[8,64,3200]{2,1,0:T(8,128)(2,1)S(1)}, u32[]{:S(2)}, u32[]{:S(2)}) async-start(bf16[8,64,3200]{2,1,0:T(8,128)(2,1)} %forward.1), calls=%async_computation.2 | async-start | bytes 6553600 | tf_op jit(solution)/shard_map/all_to_all | solution.py:286
  88.6 43.5 %all-to-all-done.2 = bf16[8,64,3200]{2,1,0:T(8,128)(2,1)S(1)} async-done(((bf16[8,64,3200]{2,1,0:T(8,128)(2,1)}), bf16[8,64,3200]{2,1,0:T(8,128)(2,1)S(1)}, u32[]{:S(2)}, u32[]{:S(2)}) %all-to-all-start.2) | async-done | bytes 3276832 | tf_op jit(solution)/shard_map/all_to_all | solution.py:286
  133.9 2.3 collective-permute-start.11
  136.2 1.3 collective-permute-start.10
  137.6 6.3 %collective-permute-done.11.refs_2_ = bf16[64,3072]{1,0:T(8,128)(2,1)S(1)} collective-permute-done((bf16[64,3072]{1,0:T(8,128)(2,1)S(1)}, bf16[64,3072]{1,0:T(8,128)(2,1)S(1)}, u32[]{:S(2)}, u32[]{:S(2)}) %collective-permute-start.11) | collective-permute-done | bytes 393248 | tf_op jit(solution)/shard_map/ppermute | solution.py:38
  143.9 3.3 %collective-permute-start.15 = (bf16[32,3072]{1,0:T(8,128)(2,1)S(1)}, bf16[32,3072]{1,0:T(8,128)(2,1)S(1)}, u32[]{:S(2)}, u32[]{:S(2)}) collective-permute-start(bf16[32,3072]{1,0:T(8,128)(2,1)S(1)} %slice.180), channel_id=1, source_target_pairs={{0,64},{64,128},{128,192},{192,0},{1,65},{65,129},{129,193},{193,1... | collective-permute-start | bytes 589832 | tf_op jit(solution)/shard_map/ppermute | solution.py:38
  147.4 1.6 collective-permute-start.14
  149.0 3.1 %collective-permute-start.13 = (bf16[64,3072]{1,0:T(8,128)(2,1)S(1)}, bf16[64,3072]{1,0:T(8,128)(2,1)S(1)}, u32[]{:S(2)}, u32[]{:S(2)}) collective-permute-start(bf16[64,3072]{1,0:T(8,128)(2,1)S(1)} %collective-permute-done.10.refs_1_), channel_id=1, source_target_pairs={{0,64},{64,128},{128,192},{192,0},{1,65},{65,129},{129,193},{193,1... | collective-permute-start | bytes 1179656 | tf_op jit(solution)/shard_map/ppermute | solution.py:38
  152.2 2.1 collective-permute-done.16
  154.3 1.6 collective-permute-start.17
  156.0 2.9 %collective-permute-done.13.refs_4_ = bf16[64,3072]{1,0:T(8,128)(2,1)S(1)} collective-permute-done((bf16[64,3072]{1,0:T(8,128)(2,1)S(1)}, bf16[64,3072]{1,0:T(8,128)(2,1)S(1)}, u32[]{:S(2)}, u32[]{:S(2)}) %collective-permute-start.13) | collective-permute-done | bytes 393248 | tf_op jit(solution)/shard_map/ppermute | solution.py:38
  158.9 5.5 %collective-permute-done.17.refs_7_ = bf16[64,3072]{1,0:T(8,128)(2,1)S(1)} collective-permute-done((bf16[64,3072]{1,0:T(8,128)(2,1)S(1)}, bf16[64,3072]{1,0:T(8,128)(2,1)S(1)}, u32[]{:S(2)}, u32[]{:S(2)}) %collective-permute-start.17) | collective-permute-done | bytes 393248 | tf_op jit(solution)/shard_map/ppermute | solution.py:38
  165.2 2.7 %collective-permute-start.18 = (bf16[64,768]{1,0:T(8,128)(2,1)S(1)}, bf16[64,768]{1,0:T(8,128)(2,1)S(1)}, u32[]{:S(2)}, u32[]{:S(2)}) collective-permute-start(bf16[64,768]{1,0:T(8,128)(2,1)S(1)} %get-tuple-element.138), channel_id=1, source_target_pairs={{0,1},{1,0},{2,3},{3,2},{4,5},{5,4},{6,7},{7,6},{8,9},{9,8},{10,11... | collective-permute-start | bytes 294920 | tf_op jit(solution)/shard_map/ppermute | solution.py:42
  168.5 8.4 %backward.1 = bf16[8,80,768]{2,1,0:T(8,128)(2,1)} custom-call(s32[8]{0:T(128)} %stack.91.s, bf16[512,768]{1,0:T(8,128)(2,1)} %bitcast.104, f32[1,768]{1,0:T(1,128)} %pad_convert_fusion.pair, bf16[64,3072]{1,0:T(8,128)(2,1)} %copy-done.4, bf16[64,3072]{1,0:T(8,128)(2,1)} %copy-done.9, bf16[64,3072]{1,0:T(8,128)(2,1)} %copy-done.5, ...), custom_call_target="tpu_custom_call" | custom-call | bytes 1048576 | tf_op jit(solution)/shard_map/backward/pallas_call | solution.py:102
  177.9 7.3 %weight_products.1 = (bf16[768,768]{1,0:T(8,128)(2,1)}, bf16[768,768]{1,0:T(8,128)(2,1)}, f32[768,768]{1,0:T(8,128)}, f32[768,768]{1,0:T(8,128)}, f32[1,3072]{1,0:T(1,128)}) custom-call(s32[8]{0:T(128)} %stack.91.s, bf16[512,768]{1,0:T(8,128)(2,1)} %bitcast.105, bf16[64,3072]{1,0:T(8,128)(2,1)} %copy-done.4, bf16[64,3072]{1,0:T(8,128)(2,1)} %copy-done.9, ...), custom_call_target="tpu_custom_call" | custom-call | bytes 1048576 | tf_op jit(solution)/shard_map/weight_products/pallas_call | solution.py:102
  185.3 3.6 %all-to-all-start.3 = ((bf16[8,80,768]{2,1,0:T(8,128)(2,1)}), bf16[8,80,768]{2,1,0:T(8,128)(2,1)S(1)}, u32[]{:S(2)}, u32[]{:S(2)}) async-start(bf16[8,80,768]{2,1,0:T(8,128)(2,1)} %backward.1), calls=%async_computation.3 | async-start | bytes 1966080 | tf_op jit(solution)/shard_map/all_to_all | solution.py:317
  188.9 3.5 %add_convert_fusion = bf16[768,768]{1,0:T(8,128)(2,1)} fusion(f32[768,768]{1,0:T(8,128)} %get-tuple-element.99, bf16[768,768]{1,0:T(8,128)(2,1)} %collective-permute-done.21), kind=kLoop, calls=%fused_computation.2 | loop fusion | flops 1769472 | bytes 4718592 | tf_op jit(solution)/shard_map/convert_element_type | solution.py:320
  192.3 1.7 collective-permute-start.22
  194.1 23.0 %all-to-all-done.3.parts = bf16[8,80,768]{2,1,0:T(8,128)(2,1)S(1)} async-done(((bf16[8,80,768]{2,1,0:T(8,128)(2,1)}), bf16[8,80,768]{2,1,0:T(8,128)(2,1)S(1)}, u32[]{:S(2)}, u32[]{:S(2)}) %all-to-all-start.3) | async-done | bytes 983072 | tf_op jit(solution)/shard_map/all_to_all | solution.py:317
  217.1 5.4 %collective-permute-done.22 = bf16[768,768]{1,0:T(8,128)(2,1)} collective-permute-done((bf16[768,768]{1,0:T(8,128)(2,1)}, bf16[768,768]{1,0:T(8,128)(2,1)}, u32[]{:S(2)}, u32[]{:S(2)}) %collective-permute-start.22) | collective-permute-done | bytes 1179680 | tf_op jit(solution)/shard_map/ppermute | solution.py:42
  222.5 2.0 collect.1
  224.5 8.4 %collective-permute-start.23 = (bf16[80,768]{1,0:T(8,128)(2,1)}, bf16[80,768]{1,0:T(8,128)(2,1)S(1)}, u32[]{:S(2)}, u32[]{:S(2)}) collective-permute-start(bf16[80,768]{1,0:T(8,128)(2,1)} %get-tuple-element.102), channel_id=1, source_target_pairs={{0,0},{1,1},{2,2},{3,3},{4,32},{5,33},{6,34},{7,35},{8,64},{9,65},... | collective-permute-start | bytes 368648 | tf_op jit(solution)/shard_map/ppermute | solution.py:51
  233.6 9.1 %collective-permute-done.23 = bf16[80,768]{1,0:T(8,128)(2,1)S(1)} collective-permute-done((bf16[80,768]{1,0:T(8,128)(2,1)}, bf16[80,768]{1,0:T(8,128)(2,1)S(1)}, u32[]{:S(2)}, u32[]{:S(2)}) %collective-permute-start.23) | collective-permute-done | bytes 122912 | tf_op jit(solution)/shard_map/ppermute | solution.py:51
  243.2 3.3 %convert_add_fusion = f32[768,768]{1,0:T(8,128)} fusion(bf16[768,768]{1,0:T(8,128)(2,1)} %collective-permute-done.22, f32[768,768]{1,0:T(8,128)S(1)} %copy-done.8, bf16[768,768]{1,0:T(8,128)(2,1)} %collective-permute-done.27), kind=kLoop, calls=%fused_computation.1 | loop fusion | flops 2359296 | bytes 7077888 | tf_op jit(solution)/shard_map/add | solution.py:341
  246.6 1.3 collective-permute-start.29
  247.9 2.2 collective-permute-start.26
  250.1 1.2 collective-permute-start.25
  253.0 2.6 collective-permute-done.25
  (121 shorter events, 14.9 us)
Async XLA Ops:
  0.6 27.3 %copy-start.1 = (bf16[768,768]{1,0:T(8,128)(2,1)S(1)}, bf16[768,768]{1,0:T(8,128)(2,1)}, u32[]{:S(2)}) copy-start(bf16[768,768]{1,0:T(8,128)(2,1)} %refs_8_) | copy-start | bytes 3538948
  3.8 23.7 %all-to-all-start = ((f32[32,16,128]{2,1,0:T(8,128)}), f32[32,16,128]{2,1,0:T(8,128)S(1)}, u32[]{:S(2)}, u32[]{:S(2)}) async-start(f32[32,16,128]{2,1,0:T(8,128)} %broadcast_in_dim.24), calls=%async_computation | async-start | bytes 524288 | tf_op jit(solution)/shard_map/all_to_all | solution.py:55
  15.5 5.0 %collective-permute-start.2 = (bf16[64,192]{1,0:T(8,128)(2,1)S(1)}, bf16[64,192]{1,0:T(8,128)(2,1)S(1)}, u32[]{:S(2)}, u32[]{:S(2)}) collective-permute-start(bf16[64,192]{1,0:T(8,128)(2,1)S(1)} %get-tuple-element.156), channel_id=1, source_target_pairs={{0,3},{1,2},{2,1},{3,0},{4,7},{5,6},{6,5},{7,4},{8,11},{9,10},{10,... | collective-permute-start | bytes 73736 | tf_op jit(solution)/shard_map/ppermute | solution.py:42
  18.6 6.0 %collective-permute-start.1 = (bf16[64,192]{1,0:T(8,128)(2,1)S(1)}, bf16[64,192]{1,0:T(8,128)(2,1)S(1)}, u32[]{:S(2)}, u32[]{:S(2)}) collective-permute-start(bf16[64,192]{1,0:T(8,128)(2,1)S(1)} %get-tuple-element.157), channel_id=1, source_target_pairs={{0,2},{1,3},{2,0},{3,1},{4,6},{5,7},{6,4},{7,5},{8,10},{9,11},{10,... | collective-permute-start | bytes 73736 | tf_op jit(solution)/shard_map/ppermute | solution.py:42
  19.0 5.7 %collective-permute-start = (bf16[64,192]{1,0:T(8,128)(2,1)S(1)}, bf16[64,192]{1,0:T(8,128)(2,1)S(1)}, u32[]{:S(2)}, u32[]{:S(2)}) collective-permute-start(bf16[64,192]{1,0:T(8,128)(2,1)S(1)} %get-tuple-element.158), channel_id=1, source_target_pairs={{0,1},{1,0},{2,3},{3,2},{4,5},{5,4},{6,7},{7,6},{8,9},{9,8},{10,11... | collective-permute-start | bytes 73736 | tf_op jit(solution)/shard_map/ppermute | solution.py:42
  27.6 19.9 %copy-start.14 = (f32[4,8,16,128]{3,1,2,0:T(8,128)}, f32[4,8,16,128]{3,1,2,0:T(8,128)S(1)}, u32[]{:S(2)}) copy-start(f32[4,8,16,128]{3,1,2,0:T(8,128)S(1)} %copy.22) | copy-start | bytes 786436
  28.0 29.6 %collective-permute-start.4 = (bf16[768,768]{1,0:T(8,128)(2,1)S(1)}, bf16[768,768]{1,0:T(8,128)(2,1)S(1)}, u32[]{:S(2)}, u32[]{:S(2)}) collective-permute-start(bf16[768,768]{1,0:T(8,128)(2,1)S(1)} %copy-done.1), channel_id=1, source_target_pairs={{0,2},{1,3},{2,0},{3,1},{4,6},{5,7},{6,4},{7,5},{8,10},{9,11},{10,... | collective-permute-start | bytes 3538952 | tf_op jit(solution)/shard_map/ppermute | solution.py:42
  30.4 16.3 %collective-permute-start.3 = (bf16[64,768]{1,0:T(8,128)(2,1)S(1)}, bf16[64,768]{1,0:T(8,128)(2,1)S(1)}, u32[]{:S(2)}, u32[]{:S(2)}) collective-permute-start(bf16[64,768]{1,0:T(8,128)(2,1)S(1)} %multiply_convert_fusion.2), channel_id=1, source_target_pairs={{0,0},{1,1},{2,2},{3,3},{4,32},{5,33},{6,34},{7,35},{8,64},{9,65},... | collective-permute-start | bytes 294920 | tf_op jit(solution)/shard_map/ppermute | solution.py:51
  47.5 23.3 %all-to-all-start.1 = ((bf16[8,64,768]{2,1,0:T(8,128)(2,1)}), bf16[8,64,768]{2,1,0:T(8,128)(2,1)S(1)}, u32[]{:S(2)}, u32[]{:S(2)}) async-start(bf16[8,64,768]{2,1,0:T(8,128)(2,1)} %broadcast_in_dim.25), calls=%async_computation.1 | async-start | bytes 1572864 | tf_op jit(solution)/shard_map/all_to_all | solution.py:55
  51.1 19.5 %collective-permute-start.5 = (bf16[768,768]{1,0:T(8,128)(2,1)S(1)}, bf16[768,768]{1,0:T(8,128)(2,1)}, u32[]{:S(2)}, u32[]{:S(2)}) collective-permute-start(bf16[768,768]{1,0:T(8,128)(2,1)S(1)} %copy-done.1), channel_id=1, source_target_pairs={{0,1},{1,0},{2,3},{3,2},{4,5},{5,4},{6,7},{7,6},{8,9},{9,8},{10,11... | collective-permute-start | bytes 3538952 | tf_op jit(solution)/shard_map/ppermute | solution.py:42
  57.6 14.3 %copy-start.2 = (bf16[768,768]{1,0:T(8,128)(2,1)}, bf16[768,768]{1,0:T(8,128)(2,1)S(1)}, u32[]{:S(2)}) copy-start(bf16[768,768]{1,0:T(8,128)(2,1)S(1)} %collective-permute-done.4.w1.refs_9_) | copy-start | bytes 3538948
  57.6 13.3 %collective-permute-start.6 = (bf16[768,768]{1,0:T(8,128)(2,1)S(1)}, bf16[768,768]{1,0:T(8,128)(2,1)}, u32[]{:S(2)}, u32[]{:S(2)}) collective-permute-start(bf16[768,768]{1,0:T(8,128)(2,1)S(1)} %collective-permute-done.4.w1.refs_9_), channel_id=1, source_target_pairs={{0,1},{1,0},{2,3},{3,2},{4,5},{5,4},{6,7},{7,6},{8,9},{9,8},{10,11... | collective-permute-start | bytes 3538952 | tf_op jit(solution)/shard_map/ppermute | solution.py:42
  59.7 6.5 %collective-permute-start.9 = (bf16[64,768]{1,0:T(8,128)(2,1)}, bf16[64,768]{1,0:T(8,128)(2,1)S(1)}, u32[]{:S(2)}, u32[]{:S(2)}) collective-permute-start(bf16[64,768]{1,0:T(8,128)(2,1)} %get-tuple-element.140), channel_id=1, source_target_pairs={{0,3},{1,2},{2,1},{3,0},{4,7},{5,6},{6,5},{7,4},{8,11},{9,10},{10,... | collective-permute-start | bytes 294920 | tf_op jit(solution)/shard_map/ppermute | solution.py:42
  60.9 5.4 %collective-permute-start.8 = (bf16[64,768]{1,0:T(8,128)(2,1)}, bf16[64,768]{1,0:T(8,128)(2,1)}, u32[]{:S(2)}, u32[]{:S(2)}) collective-permute-start(bf16[64,768]{1,0:T(8,128)(2,1)} %get-tuple-element.141), channel_id=1, source_target_pairs={{0,1},{1,0},{2,3},{3,2},{4,5},{5,4},{6,7},{7,6},{8,9},{9,8},{10,11... | collective-permute-start | bytes 294920 | tf_op jit(solution)/shard_map/ppermute | solution.py:42
  61.3 7.4 %collective-permute-start.7 = (bf16[64,768]{1,0:T(8,128)(2,1)S(1)}, bf16[64,768]{1,0:T(8,128)(2,1)}, u32[]{:S(2)}, u32[]{:S(2)}) collective-permute-start(bf16[64,768]{1,0:T(8,128)(2,1)S(1)} %get-tuple-element.142), channel_id=1, source_target_pairs={{0,2},{1,3},{2,0},{3,1},{4,6},{5,7},{6,4},{7,5},{8,10},{9,11},{10,... | collective-permute-start | bytes 294920 | tf_op jit(solution)/shard_map/ppermute | solution.py:42
  80.3 51.8 %all-to-all-start.2 = ((bf16[8,64,3200]{2,1,0:T(8,128)(2,1)}), bf16[8,64,3200]{2,1,0:T(8,128)(2,1)S(1)}, u32[]{:S(2)}, u32[]{:S(2)}) async-start(bf16[8,64,3200]{2,1,0:T(8,128)(2,1)} %forward.1), calls=%async_computation.2 | async-start | bytes 6553600 | tf_op jit(solution)/shard_map/all_to_all | solution.py:286
  133.9 34.6 %copy-start.4 = (bf16[64,3072]{1,0:T(8,128)(2,1)}, bf16[64,3072]{1,0:T(8,128)(2,1)S(1)}, u32[]{:S(2)}) copy-start(bf16[64,3072]{1,0:T(8,128)(2,1)S(1)} %get-tuple-element.91.refs_0_) | copy-start | bytes 1179652
  133.9 10.0 %collective-permute-start.11 = (bf16[64,3072]{1,0:T(8,128)(2,1)S(1)}, bf16[64,3072]{1,0:T(8,128)(2,1)S(1)}, u32[]{:S(2)}, u32[]{:S(2)}) collective-permute-start(bf16[64,3072]{1,0:T(8,128)(2,1)S(1)} %get-tuple-element.91.refs_0_), channel_id=1, source_target_pairs={{0,64},{64,128},{128,192},{192,0},{1,65},{65,129},{129,193},{193,1... | collective-permute-start | bytes 1179656 | tf_op jit(solution)/shard_map/ppermute | solution.py:38
  136.2 11.0 %collective-permute-start.12 = (bf16[64,3072]{1,0:T(8,128)(2,1)S(1)}, bf16[64,3072]{1,0:T(8,128)(2,1)S(1)}, u32[]{:S(2)}, u32[]{:S(2)}) collective-permute-start(bf16[64,3072]{1,0:T(8,128)(2,1)S(1)} %get-tuple-element.91.refs_0_), channel_id=1, source_target_pairs={{0,192},{64,0},{128,64},{192,128},{1,193},{65,1},{129,65},{193,129... | collective-permute-start | bytes 1179656 | tf_op jit(solution)/shard_map/ppermute | solution.py:38
  136.2 12.8 %collective-permute-start.10 = (bf16[64,3072]{1,0:T(8,128)(2,1)S(1)}, bf16[64,3072]{1,0:T(8,128)(2,1)S(1)}, u32[]{:S(2)}, u32[]{:S(2)}) collective-permute-start(bf16[64,3072]{1,0:T(8,128)(2,1)S(1)} %get-tuple-element.91.refs_0_), channel_id=1, source_target_pairs={{0,32},{32,0},{1,33},{33,1},{2,34},{34,2},{3,35},{35,3},{4,36},{36... | collective-permute-start | bytes 1179656 | tf_op jit(solution)/shard_map/ppermute | solution.py:38
  143.9 24.6 %copy-start.5 = (bf16[64,3072]{1,0:T(8,128)(2,1)}, bf16[64,3072]{1,0:T(8,128)(2,1)S(1)}, u32[]{:S(2)}) copy-start(bf16[64,3072]{1,0:T(8,128)(2,1)S(1)} %collective-permute-done.11.refs_2_) | copy-start | bytes 1179652
  143.9 8.2 %collective-permute-start.15 = (bf16[32,3072]{1,0:T(8,128)(2,1)S(1)}, bf16[32,3072]{1,0:T(8,128)(2,1)S(1)}, u32[]{:S(2)}, u32[]{:S(2)}) collective-permute-start(bf16[32,3072]{1,0:T(8,128)(2,1)S(1)} %slice.180), channel_id=1, source_target_pairs={{0,64},{64,128},{128,192},{192,0},{1,65},{65,129},{129,193},{193,1... | collective-permute-start | bytes 589832 | tf_op jit(solution)/shard_map/ppermute | solution.py:38
  147.3 21.2 %copy-start.6 = (bf16[64,3072]{1,0:T(8,128)(2,1)}, bf16[64,3072]{1,0:T(8,128)(2,1)S(1)}, u32[]{:S(2)}) copy-start(bf16[64,3072]{1,0:T(8,128)(2,1)S(1)} %collective-permute-done.12.refs_3_) | copy-start | bytes 1179652
  147.3 7.0 %collective-permute-start.16 = (bf16[32,3072]{1,0:T(8,128)(2,1)S(1)}, bf16[32,3072]{1,0:T(8,128)(2,1)S(1)}, u32[]{:S(2)}, u32[]{:S(2)}) collective-permute-start(bf16[32,3072]{1,0:T(8,128)(2,1)S(1)} %slice.181), channel_id=1, source_target_pairs={{0,192},{64,0},{128,64},{192,128},{1,193},{65,1},{129,65},{193,129... | collective-permute-start | bytes 589832 | tf_op jit(solution)/shard_map/ppermute | solution.py:38
  147.4 11.5 %collective-permute-start.14 = (bf16[64,3072]{1,0:T(8,128)(2,1)S(1)}, bf16[64,3072]{1,0:T(8,128)(2,1)S(1)}, u32[]{:S(2)}, u32[]{:S(2)}) collective-permute-start(bf16[64,3072]{1,0:T(8,128)(2,1)S(1)} %collective-permute-done.12.refs_3_), channel_id=1, source_target_pairs={{0,32},{32,0},{1,33},{33,1},{2,34},{34,2},{3,35},{35,3},{4,36},{36... | collective-permute-start | bytes 1179656 | tf_op jit(solution)/shard_map/ppermute | solution.py:38
  149.0 19.5 %copy-start.9 = (bf16[64,3072]{1,0:T(8,128)(2,1)}, bf16[64,3072]{1,0:T(8,128)(2,1)S(1)}, u32[]{:S(2)}) copy-start(bf16[64,3072]{1,0:T(8,128)(2,1)S(1)} %collective-permute-done.10.refs_1_) | copy-start | bytes 1179652
  149.0 9.9 %collective-permute-start.13 = (bf16[64,3072]{1,0:T(8,128)(2,1)S(1)}, bf16[64,3072]{1,0:T(8,128)(2,1)S(1)}, u32[]{:S(2)}, u32[]{:S(2)}) collective-permute-start(bf16[64,3072]{1,0:T(8,128)(2,1)S(1)} %collective-permute-done.10.refs_1_), channel_id=1, source_target_pairs={{0,64},{64,128},{128,192},{192,0},{1,65},{65,129},{129,193},{193,1... | collective-permute-start | bytes 1179656 | tf_op jit(solution)/shard_map/ppermute | solution.py:38
  154.3 14.2 %copy-start.7 = (bf16[64,3072]{1,0:T(8,128)(2,1)}, bf16[64,3072]{1,0:T(8,128)(2,1)S(1)}, u32[]{:S(2)}) copy-start(bf16[64,3072]{1,0:T(8,128)(2,1)S(1)} %constant_dynamic-update-slice_fusion.refs_6_) | copy-start | bytes 1179652
  154.3 10.1 %collective-permute-start.17 = (bf16[64,3072]{1,0:T(8,128)(2,1)S(1)}, bf16[64,3072]{1,0:T(8,128)(2,1)S(1)}, u32[]{:S(2)}, u32[]{:S(2)}) collective-permute-start(bf16[64,3072]{1,0:T(8,128)(2,1)S(1)} %constant_dynamic-update-slice_fusion.refs_6_), channel_id=1, source_target_pairs={{0,32},{32,0},{1,33},{33,1},{2,34},{34,2},{3,35},{35,3},{4,36},{36... | collective-permute-start | bytes 1179656 | tf_op jit(solution)/shard_map/ppermute | solution.py:38
  158.9 9.6 %copy-start.11 = (bf16[64,3072]{1,0:T(8,128)(2,1)}, bf16[64,3072]{1,0:T(8,128)(2,1)S(1)}, u32[]{:S(2)}) copy-start(bf16[64,3072]{1,0:T(8,128)(2,1)S(1)} %collective-permute-done.13.refs_4_) | copy-start | bytes 1179652
  158.9 9.6 %copy-start.10 = (bf16[64,3072]{1,0:T(8,128)(2,1)}, bf16[64,3072]{1,0:T(8,128)(2,1)S(1)}, u32[]{:S(2)}) copy-start(bf16[64,3072]{1,0:T(8,128)(2,1)S(1)} %collective-permute-done.14.refs_5_) | copy-start | bytes 1179652
  164.4 12.5 %collective-permute-start.20 = (bf16[64,768]{1,0:T(8,128)(2,1)S(1)}, bf16[64,768]{1,0:T(8,128)(2,1)S(1)}, u32[]{:S(2)}, u32[]{:S(2)}) collective-permute-start(bf16[64,768]{1,0:T(8,128)(2,1)S(1)} %get-tuple-element.136), channel_id=1, source_target_pairs={{0,3},{1,2},{2,1},{3,0},{4,7},{5,6},{6,5},{7,4},{8,11},{9,10},{10,... | collective-permute-start | bytes 294920 | tf_op jit(solution)/shard_map/ppermute | solution.py:42
  164.5 12.4 %collective-permute-start.19 = (bf16[64,768]{1,0:T(8,128)(2,1)S(1)}, bf16[64,768]{1,0:T(8,128)(2,1)S(1)}, u32[]{:S(2)}, u32[]{:S(2)}) collective-permute-start(bf16[64,768]{1,0:T(8,128)(2,1)S(1)} %get-tuple-element.137), channel_id=1, source_target_pairs={{0,2},{1,3},{2,0},{3,1},{4,6},{5,7},{6,4},{7,5},{8,10},{9,11},{10,... | collective-permute-start | bytes 294920 | tf_op jit(solution)/shard_map/ppermute | solution.py:42
  165.2 11.8 %collective-permute-start.18 = (bf16[64,768]{1,0:T(8,128)(2,1)S(1)}, bf16[64,768]{1,0:T(8,128)(2,1)S(1)}, u32[]{:S(2)}, u32[]{:S(2)}) collective-permute-start(bf16[64,768]{1,0:T(8,128)(2,1)S(1)} %get-tuple-element.138), channel_id=1, source_target_pairs={{0,1},{1,0},{2,3},{3,2},{4,5},{5,4},{6,7},{7,6},{8,9},{9,8},{10,11... | collective-permute-start | bytes 294920 | tf_op jit(solution)/shard_map/ppermute | solution.py:42
  185.2 3.7 %collective-permute-start.21 = (bf16[768,768]{1,0:T(8,128)(2,1)}, bf16[768,768]{1,0:T(8,128)(2,1)}, u32[]{:S(2)}, u32[]{:S(2)}) collective-permute-start(bf16[768,768]{1,0:T(8,128)(2,1)} %get-tuple-element.100), channel_id=1, source_target_pairs={{0,1},{1,0},{2,3},{3,2},{4,5},{5,4},{6,7},{7,6},{8,9},{9,8},{10,11... | collective-permute-start | bytes 3538952 | tf_op jit(solution)/shard_map/ppermute | solution.py:42
  185.3 31.8 %all-to-all-start.3 = ((bf16[8,80,768]{2,1,0:T(8,128)(2,1)}), bf16[8,80,768]{2,1,0:T(8,128)(2,1)S(1)}, u32[]{:S(2)}, u32[]{:S(2)}) async-start(bf16[8,80,768]{2,1,0:T(8,128)(2,1)} %backward.1), calls=%async_computation.3 | async-start | bytes 1966080 | tf_op jit(solution)/shard_map/all_to_all | solution.py:317
  188.8 54.2 %copy-start.15 = (f32[1,3072]{1,0:T(1,128)S(1)}, f32[1,3072]{1,0:T(1,128)}, u32[]{:S(2)}) copy-start(f32[1,3072]{1,0:T(1,128)} %get-tuple-element.108) | copy-start | bytes 36868
  188.9 54.3 %copy-start.8 = (f32[768,768]{1,0:T(8,128)S(1)}, f32[768,768]{1,0:T(8,128)}, u32[]{:S(2)}) copy-start(f32[768,768]{1,0:T(8,128)} %get-tuple-element.104) | copy-start | bytes 7077892
  192.3 30.2 %collective-permute-start.22 = (bf16[768,768]{1,0:T(8,128)(2,1)}, bf16[768,768]{1,0:T(8,128)(2,1)}, u32[]{:S(2)}, u32[]{:S(2)}) collective-permute-start(bf16[768,768]{1,0:T(8,128)(2,1)} %add_convert_fusion), channel_id=1, source_target_pairs={{0,2},{1,3},{2,0},{3,1},{4,6},{5,7},{6,4},{7,5},{8,10},{9,11},{10,... | collective-permute-start | bytes 3538952 | tf_op jit(solution)/shard_map/ppermute | solution.py:42
  194.1 49.1 %collective-permute-start.27 = (bf16[768,768]{1,0:T(8,128)(2,1)}, bf16[768,768]{1,0:T(8,128)(2,1)}, u32[]{:S(2)}, u32[]{:S(2)}) collective-permute-start(bf16[768,768]{1,0:T(8,128)(2,1)} %get-tuple-element.105), channel_id=1, source_target_pairs={{0,1},{1,0},{2,3},{3,2},{4,5},{5,4},{6,7},{7,6},{8,9},{9,8},{10,11... | collective-permute-start | bytes 3538952 | tf_op jit(solution)/shard_map/ppermute | solution.py:42
  217.1 5.4 %copy-start.3 = (bf16[8,80,768]{2,1,0:T(8,128)(2,1)}, bf16[8,80,768]{2,1,0:T(8,128)(2,1)S(1)}, u32[]{:S(2)}) copy-start(bf16[8,80,768]{2,1,0:T(8,128)(2,1)S(1)} %all-to-all-done.3.parts) | copy-start | bytes 2949124
  224.5 18.3 %collective-permute-start.23 = (bf16[80,768]{1,0:T(8,128)(2,1)}, bf16[80,768]{1,0:T(8,128)(2,1)S(1)}, u32[]{:S(2)}, u32[]{:S(2)}) collective-permute-start(bf16[80,768]{1,0:T(8,128)(2,1)} %get-tuple-element.102), channel_id=1, source_target_pairs={{0,0},{1,1},{2,2},{3,3},{4,32},{5,33},{6,34},{7,35},{8,64},{9,65},... | collective-permute-start | bytes 368648 | tf_op jit(solution)/shard_map/ppermute | solution.py:51
  243.1 3.5 %collective-permute-start.28 = (f32[1,1536]{1,0:T(1,128)S(1)}, f32[1,1536]{1,0:T(1,128)S(1)}, u32[]{:S(2)}, u32[]{:S(2)}) collective-permute-start(f32[1,1536]{1,0:T(1,128)S(1)} %slice.172), channel_id=1, source_target_pairs={{0,1},{1,0},{2,3},{3,2},{4,5},{5,4},{6,7},{7,6},{8,9},{9,8},{10,11... | collective-permute-start | bytes 18440 | tf_op jit(solution)/shard_map/ppermute | solution.py:42
  243.2 13.3 %copy-start.16 = (bf16[192]{0:T(256)(128)(2,1)S(1)}, bf16[192]{0:T(256)(128)(2,1)}, u32[]{:S(2)}) copy-start(bf16[192]{0:T(256)(128)(2,1)} %param.6) | copy-start | bytes 1156
  246.6 5.2 %collective-permute-start.29 = (f32[1,768]{1,0:T(1,128)S(1)}, f32[1,768]{1,0:T(1,128)S(1)}, u32[]{:S(2)}, u32[]{:S(2)}) collective-permute-start(f32[1,768]{1,0:T(1,128)S(1)} %slice.193), channel_id=1, source_target_pairs={{0,2},{1,3},{2,0},{3,1},{4,6},{5,7},{6,4},{7,5},{8,10},{9,11},{10,... | collective-permute-start | bytes 9224 | tf_op jit(solution)/shard_map/ppermute | solution.py:42
  247.9 5.2 %collective-permute-start.26 = (bf16[80,192]{1,0:T(8,128)(2,1)S(1)}, bf16[80,192]{1,0:T(8,128)(2,1)S(1)}, u32[]{:S(2)}, u32[]{:S(2)}) collective-permute-start(bf16[80,192]{1,0:T(8,128)(2,1)S(1)} %get-tuple-element.148), channel_id=1, source_target_pairs={{0,3},{1,2},{2,1},{3,0},{4,7},{5,6},{6,5},{7,4},{8,11},{9,10},{10,... | collective-permute-start | bytes 92168 | tf_op jit(solution)/shard_map/ppermute | solution.py:42
  250.1 5.5 %collective-permute-start.25 = (bf16[80,192]{1,0:T(8,128)(2,1)S(1)}, bf16[80,192]{1,0:T(8,128)(2,1)S(1)}, u32[]{:S(2)}, u32[]{:S(2)}) collective-permute-start(bf16[80,192]{1,0:T(8,128)(2,1)S(1)} %get-tuple-element.149), channel_id=1, source_target_pairs={{0,2},{1,3},{2,0},{3,1},{4,6},{5,7},{6,4},{7,5},{8,10},{9,11},{10,... | collective-permute-start | bytes 92168 | tf_op jit(solution)/shard_map/ppermute | solution.py:42
  251.3 4.3 %collective-permute-start.24 = (bf16[80,192]{1,0:T(8,128)(2,1)S(1)}, bf16[80,192]{1,0:T(8,128)(2,1)S(1)}, u32[]{:S(2)}, u32[]{:S(2)}) collective-permute-start(bf16[80,192]{1,0:T(8,128)(2,1)S(1)} %get-tuple-element.150), channel_id=1, source_target_pairs={{0,1},{1,0},{2,3},{3,2},{4,5},{5,4},{6,7},{7,6},{8,9},{9,8},{10,11... | collective-permute-start | bytes 92168 | tf_op jit(solution)/shard_map/ppermute | solution.py:42
  (3 other events, 6.1 us)
